TPU v7x, 256 devices: a whole 4x4x8 slice. The times are simulated.
256 devices in a mesh: dp: 32 (over x, y, core), mp: 8 (over z).
Axes of the slice: x: 4, y: 4, z: 8, core: 2. Of those that a mesh axis runs over, the one named last changes fastest.
Arguments:
- grads: bfloat16 [128, 1024, 1024], P(None, 'dp', 'mp')
- order: int32 [128], replicated, may hold values from 0 to 127, each once
- left_stat: float32 [256, 512, 1024], P(('dp', 'mp'))
- right_stat: float32 [256, 512, 1024], P(('dp', 'mp'))
- left_root: bfloat16 [256, 512, 1024], P(('dp', 'mp'))
- right_root: bfloat16 [256, 512, 1024], P(('dp', 'mp'))
Outputs:
- new_left: float32 [256, 512, 1024], P(('dp', 'mp'))
- new_right: float32 [256, 512, 1024], P(('dp', 'mp'))
- update: bfloat16 [128, 1024, 1024], P(None, 'dp', 'mp')
Inputs may be any that keep to these rules, and one draw needn't show every extreme that they name: `order`: each block number appears exactly once.
All inputs are finite; a program needn't handle non-finite values.
Results may differ from a plain program's by a relative error of at most 0.0049.
Values may be sent and summed in bfloat16 or wider, within the bound.
A program may use at most 64 MiB of HBM per device.

v0:
```python
import jax
import jax.numpy as jnp
from jax import lax
from jax.sharding import PartitionSpec as P

beta_two = 0.95
clip_rms = 0.5


def partner(value, axis, bit):
    mask = 2**bit
    pairs = [(source, source ^ mask) for source in range(lax.axis_size(axis))]
    return lax.ppermute(value, axis, pairs)


def join_halves(mine, other, half_index):
    first = jnp.where(half_index == 0, mine, other)
    second = jnp.where(half_index == 0, other, mine)
    return jnp.concatenate([first, second], axis=0)


def body(grads, order, left_stat, right_stat, left_root, right_root):
    blocks = grads.shape[0]
    n_model = lax.axis_size("mp")
    pairs = n_model // 2
    half = left_stat.shape[1]
    width = left_stat.shape[2]
    half_index = lax.axis_index("mp") % 2
    shard_sq = jnp.sum(jnp.square(grads.astype(jnp.float32)))
    total = lax.psum(shard_sq, ("dp", "mp"))
    ordered = jnp.take(grads, order, axis=0)
    owned = lax.all_to_all(ordered, "dp", split_axis=0, concat_axis=1, tiled=True)
    columns = owned.shape[2]
    pieces = owned.reshape(pairs * 2, half, columns)
    mine = lax.all_to_all(pieces, "mp", split_axis=0, concat_axis=2, tiled=True)[0]
    other = partner(mine, "mp", 0)
    full = join_halves(mine, other, half_index)
    other_root = partner(right_root[0], "mp", 0)
    root_full = join_halves(right_root[0], other_root, half_index)
    gram_left = lax.dot_general(
        mine, full, (((1,), (1,)), ((), ())), preferred_element_type=jnp.float32
    )
    my_columns = lax.dynamic_slice_in_dim(full, half_index * half, half, 1)
    gram_right = lax.dot_general(
        my_columns, full, (((0,), (0,)), ((), ())), preferred_element_type=jnp.float32
    )
    product = jnp.dot(left_root[0], full, preferred_element_type=jnp.float32).astype(jnp.bfloat16)
    precond = jnp.dot(product, root_full, preferred_element_type=jnp.float32)
    grad_sq = jnp.sum(jnp.square(full.astype(jnp.float32)))
    upd_sq = jnp.sum(precond * precond)
    upd_total = upd_sq + partner(upd_sq, "mp", 0)
    clip = jnp.minimum(
        1.0, clip_rms * jnp.sqrt(jnp.float32(blocks * width * width)) / jnp.sqrt(total + 1e-06)
    )
    new_left = beta_two * left_stat + (1.0 - beta_two) * clip * clip * gram_left[None]
    new_right = beta_two * right_stat + (1.0 - beta_two) * clip * clip * gram_right[None]
    graft = clip * jnp.sqrt(grad_sq) / jnp.sqrt(upd_total + 1e-06)
    upd_rows = (-graft * precond).astype(jnp.bfloat16)
    slabs = lax.all_to_all(upd_rows[None], "mp", split_axis=2, concat_axis=0, tiled=True)
    slabs = slabs.reshape(pairs, width, slabs.shape[2])
    slot_rows = lax.all_to_all(slabs, "dp", split_axis=1, concat_axis=0, tiled=True)
    inverse = jnp.zeros((blocks,), jnp.int32).at[order].set(jnp.arange(blocks, dtype=jnp.int32))
    update = jnp.take(slot_rows, inverse, axis=0)
    return (new_left, new_right, update)


def solution(mesh):
    return jax.shard_map(
        body,
        mesh=mesh,
        in_specs=(
            P(None, "dp", "mp"),
            P(),
            P(("dp", "mp"), None, None),
            P(("dp", "mp"), None, None),
            P(("dp", "mp"), None, None),
            P(("dp", "mp"), None, None),
        ),
        out_specs=(P(("dp", "mp"), None, None), P(("dp", "mp"), None, None), P(None, "dp", "mp")),
        check_vma=False,
    )
```

profile of v0, /device:TPU:1, one launch (start us, length us, event | category | flops | bytes accessed | tf_op | source)
XLA Modules:
  0.0 264.4 jit_solution(6560390259244584784)
XLA Ops:
  0.6 0.0 copy-start
  0.6 0.7 compare_select_fusion.1
  1.4 0.7 compare_and_fusion.1
  2.1 2.0 gather_fusion
  4.1 0.2 broadcast_select_fusion.1
  4.3 25.3 %all_to_all.63 = bf16[128,32,128]{2,1,0:T(8,128)(2,1)S(1)} all-to-all(bf16[128,32,128]{2,1,0:T(8,128)(2,1)S(1)} %broadcast_select_fusion.1), channel_id=1, replica_groups=mesh['dp'=32,'mp'=8] {'dp'}, dimensions={0} | all-to-all | bytes 2097152 | tf_op jit(solution)/shard_map/all_to_all | solution.py:32
  29.6 1.1 copy.21
  30.6 8.2 %all-to-all-start.1 = ((bf16[8,512,128]{2,1,0:T(8,128)(2,1)}), bf16[8,512,128]{2,1,0:T(8,128)(2,1)S(1)}, u32[]{:S(2)}, u32[]{:S(2)}) async-start(bf16[8,512,128]{2,1,0:T(8,128)(2,1)} %bitcast.2), calls=%async_computation.1 | async-start | bytes 2097152 | tf_op jit(solution)/shard_map/all_to_all | solution.py:35
  38.8 1.5 copy.23
  40.3 1.5 collective-permute-start.1
  41.9 26.2 %all-to-all-done.1 = bf16[8,512,128]{2,1,0:T(8,128)(2,1)S(1)} async-done(((bf16[8,512,128]{2,1,0:T(8,128)(2,1)}), bf16[8,512,128]{2,1,0:T(8,128)(2,1)S(1)}, u32[]{:S(2)}, u32[]{:S(2)}) %all-to-all-start.1) | async-done | bytes 1048608 | tf_op jit(solution)/shard_map/all_to_all | solution.py:35
  68.1 1.0 copy-done.2
  69.1 1.5 copy.22
  70.6 0.0 copy-start.1
  70.6 0.1 collective-permute-start
  70.7 2.6 %multiply_reduce_fusion.2 = f32[]{:T(128)} fusion(bf16[128,32,128]{2,1,0:T(8,128)(2,1)} %param.8), kind=kLoop, calls=%fused_computation.15 | loop fusion | flops 1572863 | bytes 1048580 | tf_op jit(solution)/shard_map/reduce_sum | solution.py:29
  73.3 79.4 %psum.7 = f32[]{:T(128)} all-reduce(f32[]{:T(128)} %multiply_reduce_fusion.2), channel_id=1, replica_groups=mesh['dp'=32,'mp'=8] {'dp','mp'}, use_global_device_ids=true, to_apply=%region_1.2 | all-reduce | flops 1 | bytes 8 | tf_op jit(solution)/shard_map/psum | solution.py:30
  153.4 0.0 collective-permute-done.1
  153.4 2.7 %broadcast_select_fusion.3 = (bf16[512,1024]{0,1:T(8,128)(2,1)}, bf16[512,1024]{0,1:T(8,128)(2,1)}) fusion(bf16[512,1024]{0,1:T(8,128)(2,1)} %collective-permute-done.1, pred[]{:T(512)S(6)} %eq.4, bf16[1,512,1024]{1,2,0:T(8,128)(2,1)S(1)} %copy.23), kind=kLoop, calls=%fused_computation.23 | loop fusion | flops 1048576 | bytes 4194305 | tf_op jit(solution)/shard_map/jit(_where)/select_n | solution.py:17
  156.1 0.0 copy-done.1
  156.1 0.0 collective-permute-done
  156.1 1.7 broadcast_select_fusion.5
  157.8 1.7 multiply_reduce_fusion
  160.2 5.9 %multiply_reduce_fusion.1 = (f32[]{:T(128)}, f32[512,1024]{1,0:T(8,128)}) fusion(bf16[512,1024]{0,1:T(8,128)(2,1)} %get-tuple-element.5, bf16[512,1024]{0,1:T(8,128)(2,1)} %get-tuple-element.4, bf16[1,512,1024]{2,1,0:T(8,128)(2,1)S(1)} %copy-done, bf16[512,1024]{0,1:T(8,128)(2,1)S(1)} %get-tuple-element.7, bf16[512,1024]{0,1:T(8,128)(2,1)S(1)} %get-tuple-element.6), kind=kOutput, calls=%fused_computation.14 | convolution fusion | flops 2157445120 | bytes 7340036 | tf_op jit(solution)/shard_map/dot_general | solution.py:48
  166.1 1.5 collective-permute-start.2
  167.6 1.2 collective-permute-done.2
  170.3 2.8 %fusion.4 = bf16[1,512,1024]{2,1,0:T(8,128)(2,1)} fusion(f32[512,1024]{1,0:T(8,128)} %get-tuple-element.9, f32[]{:T(128)S(6)} %neg.3), kind=kLoop, calls=%fused_computation.17 | loop fusion | flops 1048576 | bytes 3145732 | tf_op jit(solution)/shard_map/broadcast_in_dim | solution.py:59
  173.1 6.0 %copy.24 = bf16[1,512,1024]{1,0,2:T(2,128)(2,1)} copy(bf16[1,512,1024]{2,1,0:T(8,128)(2,1)} %fusion.4) | data formatting | bytes 2097152 | tf_op jit(solution)/shard_map/broadcast_in_dim | solution.py:59
  179.1 0.6 broadcast.24
  179.6 9.0 %reduce = bf16[1024,512]{1,0:T(8,128)(2,1)} reduce(bf16[1024,1,512]{2,1,0:T(2,128)(2,1)} %bitcast.41, bf16[]{:T(256)} %broadcast.24), dimensions={1}, to_apply=%bitcast.32.reduce_sub_computation | reduce | bytes 2097154
  188.7 2.6 reshape.57
  191.3 4.6 %all-to-all-start.2 = ((bf16[8,2,32768]{2,1,0:T(2,128)(2,1)}), bf16[8,2,32768]{2,1,0:T(2,128)(2,1)}, u32[]{:S(2)}, u32[]{:S(2)}) async-start(bf16[8,2,32768]{2,1,0:T(2,128)(2,1)} %reshape.57), calls=%async_computation.2 | async-start | bytes 2097152 | tf_op jit(solution)/shard_map/all_to_all | solution.py:59
  195.9 1.0 scatter_custom_fusion
  196.9 28.3 %all-to-all-done.2 = bf16[8,2,32768]{2,1,0:T(2,128)(2,1)} async-done(((bf16[8,2,32768]{2,1,0:T(2,128)(2,1)}), bf16[8,2,32768]{2,1,0:T(2,128)(2,1)}, u32[]{:S(2)}, u32[]{:S(2)}) %all-to-all-start.2) | async-done | bytes 1048608 | tf_op jit(solution)/shard_map/all_to_all | solution.py:59
  225.2 5.8 %reshape.58 = bf16[1024,1,512]{2,1,0:T(2,128)(2,1)} reshape(bf16[8,2,32768]{2,1,0:T(2,128)(2,1)} %all-to-all-done.2) | data formatting | bytes 2097152
  230.9 2.8 %copy.29 = bf16[1,512,1024]{1,2,0:T(8,128)(2,1)} copy(bf16[1,512,1024]{1,0,2:T(2,128)(2,1)} %bitcast.40) | data formatting | bytes 2097152
  233.8 2.3 copy.25
  236.0 3.1 %copy.26 = bf16[4,1024,128]{2,0,1:T(4,128)(2,1)} copy(bf16[4,1024,128]{2,1,0:T(8,128)(2,1)} %bitcast.47) | data formatting | bytes 2097152 | tf_op jit(solution)/shard_map/reshape | solution.py:60
  239.1 4.7 %all-to-all-start.3 = ((bf16[4,1024,128]{2,0,1:T(4,128)(2,1)}), bf16[4,1024,128]{2,0,1:T(4,128)(2,1)}, u32[]{:S(2)}, u32[]{:S(2)}) async-start(bf16[4,1024,128]{2,0,1:T(4,128)(2,1)} %copy.26), calls=%async_computation.3 | async-start | bytes 2097152 | tf_op jit(solution)/shard_map/all_to_all | solution.py:61
  243.9 0.0 copy-start.3
  243.9 4.6 %bitcast_add_fusion.1 = f32[1,512,1024]{2,1,0:T(8,128)} fusion(f32[1,512,1024]{2,1,0:T(8,128)} %param.10, bf16[512,1024]{0,1:T(8,128)(2,1)} %bitcast.39, f32[]{:T(128)S(6)} %mul.47, bf16[512,1024]{0,1:T(8,128)(2,1)S(1)} %get-tuple-element.7, bf16[512,1024]{0,1:T(8,128)(2,1)S(1)} %get-tuple-element.6), kind=kOutput, calls=%fused_computation.12 | convolution fusion | flops 1079508992 | bytes 7340036 | tf_op jit(solution)/shard_map/dot_general | solution.py:40
  248.6 0.0 copy-done.3
  248.6 2.6 bitcast_add_fusion
  251.2 9.7 %all-to-all-done.3 = bf16[4,1024,128]{2,0,1:T(4,128)(2,1)} async-done(((bf16[4,1024,128]{2,0,1:T(4,128)(2,1)}), bf16[4,1024,128]{2,0,1:T(4,128)(2,1)}, u32[]{:S(2)}, u32[]{:S(2)}) %all-to-all-start.3) | async-done | bytes 1048608 | tf_op jit(solution)/shard_map/all_to_all | solution.py:61
  260.9 1.4 copy.27
  262.3 0.1 copy.28
  262.4 0.8 gather_fusion.1
  263.2 1.2 broadcast_select_fusion
  (7 shorter events, 0.0 us)
Async XLA Ops:
  0.6 159.6 %copy-start = (bf16[1,512,1024]{2,1,0:T(8,128)(2,1)S(1)}, bf16[1,512,1024]{2,1,0:T(8,128)(2,1)}, u32[]{:S(2)}) copy-start(bf16[1,512,1024]{2,1,0:T(8,128)(2,1)} %param.12) | copy-start | bytes 3145732
  30.6 37.5 %all-to-all-start.1 = ((bf16[8,512,128]{2,1,0:T(8,128)(2,1)}), bf16[8,512,128]{2,1,0:T(8,128)(2,1)S(1)}, u32[]{:S(2)}, u32[]{:S(2)}) async-start(bf16[8,512,128]{2,1,0:T(8,128)(2,1)} %bitcast.2), calls=%async_computation.1 | async-start | bytes 2097152 | tf_op jit(solution)/shard_map/all_to_all | solution.py:35
  40.3 113.1 %collective-permute-start.1 = (bf16[512,1024]{0,1:T(8,128)(2,1)S(1)}, bf16[512,1024]{0,1:T(8,128)(2,1)}, u32[]{:S(2)}, u32[]{:S(2)}) collective-permute-start(bf16[512,1024]{0,1:T(8,128)(2,1)S(1)} %bitcast.42), channel_id=1, source_target_pairs={{0,1},{1,0},{2,3},{3,2},{4,5},{5,4},{6,7},{7,6},{8,9},{9,8},{10,11... | collective-permute-start | bytes 3145736 | tf_op jit(solution)/shard_map/ppermute | solution.py:13
  68.1 1.0 copy-start.2
  70.6 85.6 %copy-start.1 = (bf16[1,512,8,128]{1,3,2,0:T(8,128)(2,1)}, bf16[1,512,8,128]{1,3,2,0:T(8,128)(2,1)S(1)}, u32[]{:S(2)}) copy-start(bf16[1,512,8,128]{1,3,2,0:T(8,128)(2,1)S(1)} %copy.22) | copy-start | bytes 3145732
  70.6 85.5 %collective-permute-start = (bf16[512,1024]{0,1:T(8,128)(2,1)S(1)}, bf16[512,1024]{0,1:T(8,128)(2,1)}, u32[]{:S(2)}, u32[]{:S(2)}) collective-permute-start(bf16[512,1024]{0,1:T(8,128)(2,1)S(1)} %bitcast.38), channel_id=1, source_target_pairs={{0,1},{1,0},{2,3},{3,2},{4,5},{5,4},{6,7},{7,6},{8,9},{9,8},{10,11... | collective-permute-start | bytes 3145736 | tf_op jit(solution)/shard_map/ppermute | solution.py:13
  166.1 2.7 %collective-permute-start.2 = (f32[]{:T(128)}, f32[]{:T(128)}, u32[]{:S(2)}, u32[]{:S(2)}) collective-permute-start(f32[]{:T(128)} %get-tuple-element.8), channel_id=1, source_target_pairs={{0,1},{1,0},{2,3},{3,2},{4,5},{5,4},{6,7},{7,6},{8,9},{9,8},{10,11... | collective-permute-start | bytes 20 | tf_op jit(solution)/shard_map/ppermute | solution.py:13
  191.3 33.9 %all-to-all-start.2 = ((bf16[8,2,32768]{2,1,0:T(2,128)(2,1)}), bf16[8,2,32768]{2,1,0:T(2,128)(2,1)}, u32[]{:S(2)}, u32[]{:S(2)}) async-start(bf16[8,2,32768]{2,1,0:T(2,128)(2,1)} %reshape.57), calls=%async_computation.2 | async-start | bytes 2097152 | tf_op jit(solution)/shard_map/all_to_all | solution.py:59
  239.1 21.8 %all-to-all-start.3 = ((bf16[4,1024,128]{2,0,1:T(4,128)(2,1)}), bf16[4,1024,128]{2,0,1:T(4,128)(2,1)}, u32[]{:S(2)}, u32[]{:S(2)}) async-start(bf16[4,1024,128]{2,0,1:T(4,128)(2,1)} %copy.26), calls=%async_computation.3 | async-start | bytes 2097152 | tf_op jit(solution)/shard_map/all_to_all | solution.py:61
  243.9 4.7 %copy-start.3 = (f32[1,512,1024]{2,1,0:T(8,128)S(1)}, f32[1,512,1024]{2,1,0:T(8,128)}, u32[]{:S(2)}) copy-start(f32[1,512,1024]{2,1,0:T(8,128)} %param.11) | copy-start | bytes 6291460
where the time goes:
time: 265 us; the launch traced here: 264 us
  blocking collectives  105 us (40%)
  waiting for transfers between devices  65.5 us (25%)
  local copies, waits for them, and re-layouts  33.4 us (13%)
  other arithmetic  23.4 us (9%)
  starting transfers between devices  20.6 us (8%)
  matrix products  13.2 us (5%)
  between operations  3.61 us (1%)
    psum x1, blocking collectives, body(): total = lax.psum(shard_sq, ('dp', 'mp'))  79.4 us
    all_to_all x1, waiting for transfers between devices, body(): lax.all_to_all(upd_rows[None], 'mp', split_axis=2, concat_axis=0, tiled=T...  28.3 us
    all_to_all x1, waiting for transfers between devices, body(): lax.all_to_all(pieces, 'mp', split_axis=0, concat_axis=2, tiled=True)[0]  26.2 us
    all_to_all x1, blocking collectives, body(): lax.all_to_all(ordered, 'dp', split_axis=0, concat_axis=1, tiled=True)  25.3 us
    unnamed x13, local copies, waits for them, and re-layouts  14.3 us
    all_to_all x1, waiting for transfers between devices, body(): lax.all_to_all(slabs, 'dp', split_axis=1, concat_axis=0, tiled=True)  9.71 us
    unnamed x1, other arithmetic  9.05 us
    all_to_all x1, starting transfers between devices, body(): lax.all_to_all(pieces, 'mp', split_axis=0, concat_axis=2, tiled=True)[0]  8.19 us
  transfers between devices with their start and end apart: 6, of which 4 were waited for; matrix products, arithmetic and copies ran while one was open for 6% of the time, Pallas kernels for 0%

commit v1 on v0

v1 whole, which is shorter than its diff:
```python
import functools

import jax
import jax.numpy as jnp
from jax import lax
from jax.experimental import pallas as pl
from jax.experimental.pallas import tpu as pltpu
from jax.sharding import PartitionSpec as P

MESH = pl.DeviceIdType.MESH
F32 = jnp.float32
BF16 = jnp.bfloat16
beta_two = 0.95
clip_rms = 0.5


def fold(x):
    x = x.astype(F32)
    return jnp.sum((x * x).reshape(-1, 8, 128), axis=0)


def everything(x):
    return jnp.sum(jnp.sum(x, axis=0, keepdims=True), axis=1, keepdims=True)


def kernel(
    nd,
    nm,
    order_in,
    grads_in,
    left_stat,
    right_stat,
    left_root,
    right_root,
    new_left,
    new_right,
    u_in,
    scales,
    order,
    grads,
    tiles,
    slabs,
    full,
    lroot,
    rroot,
    acc,
    last_a,
    u_out,
    sq_dp,
    sq_mine,
    sq_mp,
    g_sq,
    sums,
    load_sem,
    slab_sem,
    tile_sem,
    forward_sem,
    root_sem,
    sq_send_sem,
    sq_recv_sem,
    sum_send_sem,
    sum_recv_sem,
    u_send_sem,
    u_recv_sem,
    ready_sem,
):
    blocks, rows, cols = grads.shape
    half, width = lroot.shape
    pairs = nm // 2
    d = lax.axis_index("dp")
    m = lax.axis_index("mp")
    h = m % 2
    pair = m // 2
    sigma = 2 * h - 1
    partner = m - sigma
    per_half = nd // 2
    my_rows = pl.ds(pl.multiple_of(h * half, half), half)

    def place(offset):
        return (m + offset + 2 * nm) % nm

    first_loads = [
        pltpu.make_async_copy(order_in.at[0], order, load_sem.at[4]),
        pltpu.make_async_copy(grads_in, grads, load_sem.at[5]),
    ]
    for load in first_loads:
        load.start()

    barrier = pltpu.get_barrier_semaphore()

    def greet(k, carry):
        pl.semaphore_signal(barrier, inc=1, device_id=((d + k) % nd, m), device_id_type=MESH)
        return carry

    lax.fori_loop(1, nd, greet, 0)
    for k in range(1, nm):
        pl.semaphore_signal(barrier, inc=1, device_id=(d, (m + k) % nm), device_id_type=MESH)

    loads = [
        pltpu.make_async_copy(left_root.at[0], lroot, load_sem.at[0]),
        pltpu.make_async_copy(right_root.at[0], rroot.at[my_rows], load_sem.at[1]),
        pltpu.make_async_copy(left_stat, new_left, load_sem.at[2]),
        pltpu.make_async_copy(right_stat, new_right, load_sem.at[3]),
    ]

    pl.semaphore_wait(barrier, nd - 1 + nm - 1)
    for k in range(1, nm):
        pl.semaphore_signal(ready_sem, inc=1, device_id=(d, (m + k) % nm), device_id_type=MESH)

    part_rows = half // 4

    def root_copy(n):
        return pltpu.make_async_remote_copy(
            src_ref=right_root.at[0, pl.ds(n * part_rows, part_rows)],
            dst_ref=rroot.at[pl.ds(pl.multiple_of(h * half + n * part_rows, part_rows), part_rows)],
            send_sem=root_sem.at[0],
            recv_sem=root_sem.at[1],
            device_id=(d, partner),
            device_id_type=MESH,
        )

    root_copy(0).start()
    for load in loads:
        load.start()

    targets = [place(3 * sigma), place(-2 * sigma), place(sigma), m]

    def tile_copy(there, target):
        return pltpu.make_async_remote_copy(
            src_ref=tiles.at[pairs * there + target // 2],
            dst_ref=slabs.at[m, pl.ds(pl.multiple_of(d * rows, rows), rows)],
            send_sem=tile_sem,
            recv_sem=slab_sem.at[m],
            device_id=(there, target),
            device_id_type=MESH,
        )

    def arrange(there, total):
        for p in range(pairs):
            s = pairs * there + p
            tile = grads[order[s]]
            tiles[s] = tile
            total = total + fold(tile)
        return total

    for load in first_loads:
        load.wait()
    pl.semaphore_wait(ready_sem, nm - 1)
    total = arrange(d, jnp.zeros((8, 128), F32))
    for target in targets[:3]:
        tile_copy(d, target).start()
    pltpu.make_async_copy(
        tiles.at[pairs * d + pair],
        slabs.at[m, pl.ds(pl.multiple_of(d * rows, rows), rows)],
        slab_sem.at[m],
    ).start()

    def send_tiles(k, total):
        there = (d + k) % nd
        total = arrange(there, total)
        for target in targets:
            tile_copy(there, target).start()
        return total

    sq_dp[d] = lax.fori_loop(1, nd, send_tiles, total)

    for n in range(1, 4):
        root_copy(n).start()

    def send_sq(k, carry):
        pltpu.make_async_remote_copy(
            src_ref=sq_dp.at[d],
            dst_ref=sq_dp.at[d],
            send_sem=sq_send_sem.at[0],
            recv_sem=sq_recv_sem.at[0],
            device_id=((d + k) % nd, m),
            device_id_type=MESH,
        ).start()
        return carry

    lax.fori_loop(1, nd, send_sq, 0)
    some = sq_dp.at[pl.ds(0, nd - 1)]
    pltpu.make_async_copy(some, some, sq_recv_sem.at[0]).wait()
    sq_mine[...] = jnp.sum(sq_dp[...], axis=0)
    sq_mp[m] = sq_mine[...]
    for k in range(1, nm):
        pltpu.make_async_remote_copy(
            src_ref=sq_mine,
            dst_ref=sq_mp.at[m],
            send_sem=sq_send_sem.at[1],
            recv_sem=sq_recv_sem.at[1],
            device_id=(d, (m + k) % nm),
            device_id_type=MESH,
        ).start()

    def wait_slab(k):
        pltpu.make_async_copy(slabs.at[k], slabs.at[k], slab_sem.at[k]).wait()

    def forward(k):
        return pltpu.make_async_remote_copy(
            src_ref=slabs.at[k],
            dst_ref=slabs.at[k],
            send_sem=forward_sem.at[k],
            recv_sem=slab_sem.at[k],
            device_id=(d, partner),
            device_id_type=MESH,
        )

    for j in range(pairs):
        k = place(j * sigma)
        wait_slab(k)
        forward(k).start()

    loads[0].wait()
    loads[1].wait()
    pltpu.make_async_copy(lroot, lroot, root_sem.at[1]).wait()
    acc[...] = jnp.zeros_like(acc)
    g_sq[...] = jnp.zeros_like(g_sq)

    def through_left(k):
        slab = slabs[k]
        g_sq[...] += fold(slab)
        return jnp.dot(lroot[...], slab, preferred_element_type=F32).astype(BF16)

    def right_rows(k):
        return pl.ds(pl.multiple_of(k * cols, cols), cols)

    def use_slab(k):
        a = through_left(k)
        acc[...] += jnp.dot(a, rroot[right_rows(k)], preferred_element_type=F32)

    def near(j, carry):
        use_slab(place(j * sigma))
        return carry

    def far(j, carry):
        k = place(-(j + 1) * sigma)
        wait_slab(k)
        use_slab(k)
        return carry

    lax.fori_loop(0, pairs, near, 0)
    lax.fori_loop(0, pairs - 1, far, 0)
    last = place(-pairs * sigma)
    wait_slab(last)
    last_a[...] = through_left(last)
    step = 2 * cols

    def finish(n, total):
        part = pl.ds(pl.multiple_of(n * step, step), step)
        u = acc[:, part] + jnp.dot(
            last_a[...], rroot[right_rows(last), part], preferred_element_type=F32
        )
        u_out[2 * n] = u[:, :cols].astype(BF16)
        u_out[2 * n + 1] = u[:, cols:].astype(BF16)
        return total + fold(u[:, :cols]) + fold(u[:, cols:])

    u_sq = lax.fori_loop(0, pairs, finish, jnp.zeros((8, 128), F32))

    row = lax.broadcasted_iota(jnp.int32, (8, 128), 0)
    sums[m] = jnp.where(row < 4, everything(u_sq), everything(g_sq[...]))
    for k in range(1, nm):
        pltpu.make_async_remote_copy(
            src_ref=sums.at[m],
            dst_ref=sums.at[m],
            send_sem=sum_send_sem.at[0],
            recv_sem=sum_recv_sem.at[0],
            device_id=(d, (m + k) % nm),
            device_id_type=MESH,
        ).start()

    slot = pairs * d + pair

    def u_copy(near_row, target):
        return pltpu.make_async_remote_copy(
            src_ref=u_out.at[target, pl.ds(pl.multiple_of(near_row * rows, rows), rows)],
            dst_ref=u_in.at[slot],
            send_sem=u_send_sem,
            recv_sem=u_recv_sem,
            device_id=(h * per_half + near_row, target),
            device_id_type=MESH,
        )

    own_half = d // per_half == h

    def send_u(k, carry):
        near_row = (d + k) % per_half
        for j in range(1, nm):
            u_copy(near_row, (m + j) % nm).start()
        here = jnp.logical_and(own_half, k == 0)

        @pl.when(here)
        def _():
            pltpu.make_async_copy(
                u_out.at[m, pl.ds(pl.multiple_of(near_row * rows, rows), rows)],
                u_in.at[slot],
                u_recv_sem,
            ).start()

        @pl.when(jnp.logical_not(here))
        def _():
            u_copy(near_row, m).start()

        return carry

    lax.fori_loop(0, per_half // 2, send_u, 0)

    some_mp = sq_mp.at[pl.ds(0, nm - 1)]
    pltpu.make_async_copy(some_mp, some_mp, sq_recv_sem.at[1]).wait()
    total_sq = everything(jnp.sum(sq_mp[...], axis=0))
    clip = jnp.minimum(1.0, clip_rms * jnp.sqrt(F32(blocks * width * width)) / jnp.sqrt(total_sq + 1e-06))
    coefficient = (1.0 - beta_two) * clip * clip
    pltpu.make_async_copy(some_mp, some_mp, sum_recv_sem.at[0]).wait()
    mine = jnp.zeros((8, 128), F32)
    for p in range(pairs):
        u_total = sums[2 * p, 0:1] + sums[2 * p + 1, 0:1]
        scale = -(clip * jnp.sqrt(sums[2 * p, 4:5]) / jnp.sqrt(u_total + 1e-06))
        mine = jnp.where(row == p, scale, mine)
    scales[d] = mine

    def send_scales(k, carry):
        pltpu.make_async_remote_copy(
            src_ref=scales.at[d],
            dst_ref=scales.at[d],
            send_sem=sum_send_sem.at[1],
            recv_sem=sum_recv_sem.at[1],
            device_id=((d + k) % nd, m),
            device_id_type=MESH,
        ).start()
        return carry

    lax.fori_loop(1, nd, send_scales, 0)
    lax.fori_loop(per_half // 2, per_half, send_u, 0)

    for k in range(nm):
        full[:, k * cols : (k + 1) * cols] = slabs[k]
    loads[2].wait()

    def left_gram(n, carry):
        part = pl.ds(pl.multiple_of(n * step, step), step)
        gram = lax.dot_general(
            full[my_rows], full[part], (((1,), (1,)), ((), ())), preferred_element_type=F32
        )
        new_left[0, :, part] = beta_two * new_left[0, :, part] + coefficient * gram
        return carry

    lax.fori_loop(0, width // step, left_gram, 0)
    loads[3].wait()

    def right_gram(n, carry):
        part = pl.ds(pl.multiple_of(n * step, step), step)
        gram = lax.dot_general(
            full[:, my_rows], full[:, part], (((0,), (0,)), ((), ())), preferred_element_type=F32
        )
        new_right[0, :, part] = beta_two * new_right[0, :, part] + coefficient * gram
        return carry

    lax.fori_loop(0, width // step, right_gram, 0)

    sent = tiles.at[pl.ds(0, blocks - 1)]
    pltpu.make_async_copy(sent, sent, tile_sem).wait()
    pltpu.make_async_copy(lroot, lroot, root_sem.at[0]).wait()
    pltpu.make_async_copy(some, some, sq_send_sem.at[0]).wait()
    pltpu.make_async_copy(some_mp, some_mp, sq_send_sem.at[1]).wait()
    pltpu.make_async_copy(some_mp, some_mp, sum_send_sem.at[0]).wait()
    pltpu.make_async_copy(some, some, sum_send_sem.at[1]).wait()
    for j in range(pairs):
        forward(place(j * sigma)).wait_send()

    @pl.when(own_half)
    def _():
        pltpu.make_async_copy(sent, sent, u_send_sem).wait()

    @pl.when(jnp.logical_not(own_half))
    def _():
        pltpu.make_async_copy(tiles, tiles, u_send_sem).wait()

    pltpu.make_async_copy(some, some, sum_recv_sem.at[1]).wait()
    pltpu.make_async_copy(u_in, u_in, u_recv_sem).wait()


def finish_kernel(order_in, left, right, tiles, scales, new_left, new_right, update, order, arranged, sem):
    blocks = tiles.shape[0]
    pairs = blocks // scales.shape[0]
    order_copy = pltpu.make_async_copy(order_in.at[0], order, sem.at[0])
    order_copy.start()
    stores = [
        pltpu.make_async_copy(left, new_left, sem.at[1]),
        pltpu.make_async_copy(right, new_right, sem.at[2]),
    ]
    for store in stores:
        store.start()
    order_copy.wait()

    def give(there, carry):
        for p in range(pairs):
            s = pairs * there + p
            arranged[order[s]] = (tiles[s].astype(F32) * scales[there, p : p + 1]).astype(BF16)
        return carry

    lax.fori_loop(0, scales.shape[0], give, 0, unroll=2)
    last = pltpu.make_async_copy(arranged, update, sem.at[3])
    last.start()
    last.wait()
    for store in stores:
        store.wait()


def body(nd, nm, grads, order, left_stat, right_stat, left_root, right_root):
    blocks, rows, cols = grads.shape
    _, half, width = left_stat.shape
    vmem = pl.BlockSpec(memory_space=pltpu.VMEM)
    half_shape = left_stat.shape
    hbm = pl.BlockSpec(memory_space=pltpu.HBM)
    dma = pltpu.SemaphoreType.DMA
    operands = [order.reshape(1, blocks), grads, left_stat, right_stat, left_root, right_root]
    operands = [pltpu.with_memory_space_constraint(x, pltpu.HBM) for x in operands]
    products = 4 * half * width * width
    results = pl.pallas_call(
        functools.partial(kernel, nd, nm),
        out_shape=(
            pltpu.VMEM(left_stat.shape, F32),
            pltpu.VMEM(right_stat.shape, F32),
            pltpu.VMEM(grads.shape, BF16),
            pltpu.VMEM((nd, 8, 128), F32),
        ),
        in_specs=[hbm] * 6,
        out_specs=(vmem, vmem, vmem, vmem),
        scratch_shapes=[
            pltpu.SMEM((blocks,), jnp.int32),
            pltpu.VMEM((blocks, rows, cols), BF16),
            pltpu.VMEM((blocks, rows, cols), BF16),
            pltpu.VMEM((nm, width, cols), BF16),
            pltpu.VMEM((width, width), BF16),
            pltpu.VMEM((half, width), BF16),
            pltpu.VMEM((width, width), BF16),
            pltpu.VMEM((half, width), F32),
            pltpu.VMEM((half, cols), BF16),
            pltpu.VMEM((nm, half, cols), BF16),
            pltpu.VMEM((nd, 8, 128), F32),
            pltpu.VMEM((8, 128), F32),
            pltpu.VMEM((nm, 8, 128), F32),
            pltpu.VMEM((8, 128), F32),
            pltpu.VMEM((nm, 8, 128), F32),
            dma((6,)),
            dma((nm,)),
            dma,
            dma((nm,)),
            dma((2,)),
            dma((2,)),
            dma((2,)),
            dma((2,)),
            dma((2,)),
            dma,
            dma,
            pltpu.SemaphoreType.REGULAR,
        ],
        compiler_params=pltpu.CompilerParams(
            collective_id=0, has_side_effects=True, vmem_limit_bytes=48 * 1024 * 1024
        ),
        cost_estimate=pl.CostEstimate(
            flops=2 * products, bytes_accessed=12 * half * width * 2, transcendentals=0
        ),
        name="step",
    )(*operands)
    return pl.pallas_call(
        finish_kernel,
        out_shape=(
            pltpu.HBM(half_shape, F32),
            pltpu.HBM(half_shape, F32),
            pltpu.HBM(grads.shape, BF16),
        ),
        in_specs=[hbm, vmem, vmem, vmem, vmem],
        out_specs=(hbm, hbm, hbm),
        scratch_shapes=[
            pltpu.SMEM((blocks,), jnp.int32),
            pltpu.VMEM(grads.shape, BF16),
            dma((4,)),
        ],
        compiler_params=pltpu.CompilerParams(vmem_limit_bytes=8 * 1024 * 1024),
        cost_estimate=pl.CostEstimate(flops=0, bytes_accessed=10 * half * width, transcendentals=0),
        name="finish",
    )(operands[0], *results)


def solution(mesh):
    owned = P(("dp", "mp"), None, None)
    return jax.shard_map(
        functools.partial(body, mesh.shape["dp"], mesh.shape["mp"]),
        mesh=mesh,
        in_specs=(P(None, "dp", "mp"), P(), owned, owned, owned, owned),
        out_specs=(owned, owned, P(None, "dp", "mp")),
        check_vma=False,
    )
```

time: 265 us -> 102 us (0.38)
  blocking collectives: 105 us -> 0 us
  Pallas kernels: 0 us -> 102 us
  waiting for transfers between devices: 65.5 us -> 0 us
  local copies, waits for them, and re-layouts: 33.4 us -> 0 us
  other arithmetic: 23.4 us -> 0 us
  starting transfers between devices: 20.6 us -> 0 us
  matrix products: 13.2 us -> 0 us
  between operations: 3.61 us -> 0.64 us
    pallas_call x0 -> x2, Pallas kernels: none -> 102 us  [the longest x1 99.2 us: body(): pl.pallas_call(functools.partial(kernel, nd, nm), out_shape=(pltpu.VMEM(l...]
    psum x1 -> x0, blocking collectives: 79.4 us -> none  [body(): total = lax.psum(shard_sq, ('dp', 'mp'))]
    all_to_all x3 -> x0, waiting for transfers between devices: 64.2 us -> none  [the longest x1 28.3 us: body(): lax.all_to_all(upd_rows[None], 'mp', split_axis=2, concat_axis=0, tiled=T...]
    all_to_all x1 -> x0, blocking collectives: 25.3 us -> none  [body(): lax.all_to_all(ordered, 'dp', split_axis=0, concat_axis=1, tiled=True)]
    all_to_all x3 -> x0, starting transfers between devices: 17.5 us -> none  [the longest x1 8.19 us: body(): lax.all_to_all(pieces, 'mp', split_axis=0, concat_axis=2, tiled=True)[0]]
    unnamed x13 -> x0, local copies, waits for them, and re-layouts: 14.3 us -> none
    dot_general x3 -> x0, matrix products: 13.2 us -> none  [the longest x1 5.94 us: body(): precond = jnp.dot(product, root_full, preferred_element_type=jnp.float32)]
    unnamed x1 -> x0, other arithmetic: 9.05 us -> none
  transfers between devices with their start and end apart: 6 -> 0, of which waited for: 4 -> 0; matrix products, arithmetic and copies ran while one was open for 6% -> 0% of each run, Pallas kernels for 0% -> 0%
where the time goes in v1:
time: 102 us
  Pallas kernels  102 us (100%)
    pallas_call x1, Pallas kernels, body(): pl.pallas_call(functools.partial(kernel, nd, nm), out_shape=(pltpu.VMEM(l...  99.2 us
    pallas_call x1, Pallas kernels, body(): pl.pallas_call(finish_kernel, out_shape=(pltpu.HBM(half_shape, F32), pltp...  2.39 us

profile of v1, /device:TPU:1, one launch (start us, length us, event | category | flops | bytes accessed | tf_op | source)
XLA Modules:
  0.0 102.2 jit_solution(2720019279729012099)
XLA Ops:
  0.6 99.2 %step.1 = (f32[1,512,1024]{2,1,0:T(8,128)S(1)}, f32[1,512,1024]{2,1,0:T(8,128)S(1)}, bf16[128,32,128]{2,1,0:T(8,128)(2,1)S(1)}, f32[32,8,128]{2,1,0:T(8,128)S(1)}) custom-call(s32[1,128]{1,0:T(1,128)} %bitcast.1, bf16[128,32,128]{2,1,0:T(8,128)(2,1)} %grads_in.1, f32[1,512,1024]{2,1,0:T(8,128)} %left_stat.1, f32[1,512,1024]{2,1,0:T(8,128)} %right_stat.1, ...), custom_call_target="tpu_custom_call" | custom-call | flops 4294967296 | bytes 12582912 | tf_op jit(solution)/shard_map/step/pallas_call | solution.py:419
  99.8 2.4 %finish.1 = (f32[1,512,1024]{2,1,0:T(8,128)}, f32[1,512,1024]{2,1,0:T(8,128)}, bf16[128,32,128]{2,1,0:T(8,128)(2,1)}) custom-call(s32[1,128]{1,0:T(1,128)} %bitcast.2, f32[1,512,1024]{2,1,0:T(8,128)S(1)} %get-tuple-element.7.left, f32[1,512,1024]{2,1,0:T(8,128)S(1)} %get-tuple-element.8.right, bf16[128,32,128]{2,1,0:T(8,128)(2,1)S(1)} %get-tuple-element.9.tiles, ...), custom_call_target="tpu_custom_call" | custom-call | bytes 5242880 | tf_op jit(solution)/shard_map/finish/pallas_call | solution.py:466

commit v2 on v1

--- a/solution.py
+++ b/solution.py
@@ -46,6 +46,7 @@
     acc,
     last_a,
     u_out,
+    relay,
     sq_dp,
     sq_mine,
     sq_mp,
@@ -62,6 +63,7 @@
     sum_recv_sem,
     u_send_sem,
     u_recv_sem,
+    relay_sem,
     ready_sem,
 ):
     blocks, rows, cols = grads.shape
@@ -246,7 +248,10 @@
     last_a[...] = through_left(last)
     step = 2 * cols
 
-    def finish(n, total):
+    opposite = place(nm // 2)
+
+    def finish(i, total):
+        n = (opposite // 2 + i) % pairs
         part = pl.ds(pl.multiple_of(n * step, step), step)
         u = acc[:, part] + jnp.dot(
             last_a[...], rroot[right_rows(last), part], preferred_element_type=F32
@@ -255,7 +260,17 @@
         u_out[2 * n + 1] = u[:, cols:].astype(BF16)
         return total + fold(u[:, :cols]) + fold(u[:, cols:])
 
-    u_sq = lax.fori_loop(0, pairs, finish, jnp.zeros((8, 128), F32))
+    u_sq = finish(0, jnp.zeros((8, 128), F32))
+    relay_copy = pltpu.make_async_remote_copy(
+        src_ref=u_out.at[opposite],
+        dst_ref=relay,
+        send_sem=relay_sem.at[0],
+        recv_sem=relay_sem.at[1],
+        device_id=(d, partner),
+        device_id_type=MESH,
+    )
+    relay_copy.start()
+    u_sq = lax.fori_loop(1, pairs, finish, u_sq)
 
     row = lax.broadcasted_iota(jnp.int32, (8, 128), 0)
     sums[m] = jnp.where(row < 4, everything(u_sq), everything(g_sq[...]))
@@ -286,7 +301,8 @@
     def send_u(k, carry):
         near_row = (d + k) % per_half
         for j in range(1, nm):
-            u_copy(near_row, (m + j) % nm).start()
+            if j != nm // 2:
+                u_copy(near_row, (m + j) % nm).start()
         here = jnp.logical_and(own_half, k == 0)
 
         @pl.when(here)
@@ -304,6 +320,21 @@
         return carry
 
     lax.fori_loop(0, per_half // 2, send_u, 0)
+    relay_copy.wait_recv()
+
+    def pass_on(k, carry):
+        near_row = (d + k) % per_half
+        pltpu.make_async_remote_copy(
+            src_ref=relay.at[pl.ds(pl.multiple_of(near_row * rows, rows), rows)],
+            dst_ref=u_in.at[slot],
+            send_sem=u_send_sem,
+            recv_sem=u_recv_sem,
+            device_id=((1 - h) * per_half + near_row, (partner + nm // 2) % nm),
+            device_id_type=MESH,
+        ).start()
+        return carry
+
+    lax.fori_loop(0, per_half, pass_on, 0)
 
     some_mp = sq_mp.at[pl.ds(0, nm - 1)]
     pltpu.make_async_copy(some_mp, some_mp, sq_recv_sem.at[1]).wait()
@@ -364,6 +395,7 @@
     pltpu.make_async_copy(some_mp, some_mp, sq_send_sem.at[1]).wait()
     pltpu.make_async_copy(some_mp, some_mp, sum_send_sem.at[0]).wait()
     pltpu.make_async_copy(some, some, sum_send_sem.at[1]).wait()
+    relay_copy.wait_send()
     for j in range(pairs):
         forward(place(j * sigma)).wait_send()
 
@@ -437,6 +469,7 @@
             pltpu.VMEM((half, width), F32),
             pltpu.VMEM((half, cols), BF16),
             pltpu.VMEM((nm, half, cols), BF16),
+            pltpu.VMEM((half, cols), BF16),
             pltpu.VMEM((nd, 8, 128), F32),
             pltpu.VMEM((8, 128), F32),
             pltpu.VMEM((nm, 8, 128), F32),
@@ -453,6 +486,7 @@
             dma((2,)),
             dma,
             dma,
+            dma((2,)),
             pltpu.SemaphoreType.REGULAR,
         ],
         compiler_params=pltpu.CompilerParams(

time: 102 us -> 101 us (level)
  Pallas kernels: 102 us -> 99.9 us
    pallas_call x1, Pallas kernels: 99.2 us -> 97.6 us  [body(): pl.pallas_call(functools.partial(kernel, nd, nm), out_shape=(pltpu.VMEM(l...]
where the time goes in v2:
time: 101 us
  Pallas kernels  99.9 us (99%)
    pallas_call x1, Pallas kernels, body(): pl.pallas_call(functools.partial(kernel, nd, nm), out_shape=(pltpu.VMEM(l...  97.6 us
    pallas_call x1, Pallas kernels, body(): pl.pallas_call(finish_kernel, out_shape=(pltpu.HBM(half_shape, F32), pltp...  2.39 us

profile of v2, /device:TPU:1, one launch (start us, length us, event | category | flops | bytes accessed | tf_op | source)
XLA Modules:
  0.0 100.6 jit_solution(3304087015742221932)
XLA Ops:
  0.6 97.6 %step.1 = (f32[1,512,1024]{2,1,0:T(8,128)S(1)}, f32[1,512,1024]{2,1,0:T(8,128)S(1)}, bf16[128,32,128]{2,1,0:T(8,128)(2,1)S(1)}, f32[32,8,128]{2,1,0:T(8,128)S(1)}) custom-call(s32[1,128]{1,0:T(1,128)} %bitcast.1, bf16[128,32,128]{2,1,0:T(8,128)(2,1)} %grads_in.1, f32[1,512,1024]{2,1,0:T(8,128)} %left_stat.1, f32[1,512,1024]{2,1,0:T(8,128)} %right_stat.1, ...), custom_call_target="tpu_custom_call" | custom-call | flops 4294967296 | bytes 12582912 | tf_op jit(solution)/shard_map/step/pallas_call | solution.py:451
  98.2 2.4 %finish.1 = (f32[1,512,1024]{2,1,0:T(8,128)}, f32[1,512,1024]{2,1,0:T(8,128)}, bf16[128,32,128]{2,1,0:T(8,128)(2,1)}) custom-call(s32[1,128]{1,0:T(1,128)} %bitcast.2, f32[1,512,1024]{2,1,0:T(8,128)S(1)} %get-tuple-element.7.left, f32[1,512,1024]{2,1,0:T(8,128)S(1)} %get-tuple-element.8.right, bf16[128,32,128]{2,1,0:T(8,128)(2,1)S(1)} %get-tuple-element.9.tiles, ...), custom_call_target="tpu_custom_call" | custom-call | bytes 5242880 | tf_op jit(solution)/shard_map/finish/pallas_call | solution.py:500

commit v3 on v1

--- a/solution.py
+++ b/solution.py
@@ -46,6 +46,8 @@
     acc,
     last_a,
     u_out,
+    relay,
+    columns,
     sq_dp,
     sq_mine,
     sq_mp,
@@ -62,6 +64,9 @@
     sum_recv_sem,
     u_send_sem,
     u_recv_sem,
+    relay_sem,
+    column_send_sem,
+    column_sem,
     ready_sem,
 ):
     blocks, rows, cols = grads.shape
@@ -269,41 +274,86 @@
             device_id_type=MESH,
         ).start()
 
-    slot = pairs * d + pair
-
-    def u_copy(near_row, target):
-        return pltpu.make_async_remote_copy(
-            src_ref=u_out.at[target, pl.ds(pl.multiple_of(near_row * rows, rows), rows)],
-            dst_ref=u_in.at[slot],
-            send_sem=u_send_sem,
-            recv_sem=u_recv_sem,
-            device_id=(h * per_half + near_row, target),
-            device_id_type=MESH,
-        )
-
-    own_half = d // per_half == h
-
-    def send_u(k, carry):
-        near_row = (d + k) % per_half
+    opposite = place(nm // 2)
+    chunks = min(4, per_half)
+    chunk_places = per_half // chunks
+    chunk_rows = half // chunks
+
+    def chunk_at(i):
+        c = (i + d // 2 + d // 8) % chunks
+        return c, pl.ds(pl.multiple_of(c * chunk_rows, chunk_rows), chunk_rows)
+
+    own_copy = pltpu.make_async_copy(u_out.at[m], columns.at[h, pair], load_sem.at[6])
+    own_copy.start()
+
+    def send_columns(i, carry):
+        c, part = chunk_at(i)
+        pltpu.make_async_remote_copy(
+            src_ref=u_out.at[opposite, part],
+            dst_ref=relay.at[part],
+            send_sem=column_send_sem,
+            recv_sem=relay_sem.at[c],
+            device_id=(d, partner),
+            device_id_type=MESH,
+        ).start()
+        for j in (3, 5, 2, 6, 1, 7):
+            target = (m + j) % nm
+            pltpu.make_async_remote_copy(
+                src_ref=u_out.at[target, part],
+                dst_ref=columns.at[h, pair, part],
+                send_sem=column_send_sem,
+                recv_sem=column_sem.at[m, c],
+                device_id=(d, target),
+                device_id_type=MESH,
+            ).start()
+        return carry
+
+    lax.fori_loop(0, chunks, send_columns, 0)
+
+    def pass_on(i, carry):
+        c, part = chunk_at(i)
+        pltpu.make_async_copy(relay.at[part], relay.at[part], relay_sem.at[c]).wait()
+        pltpu.make_async_remote_copy(
+            src_ref=relay.at[part],
+            dst_ref=columns.at[1 - h, pair, part],
+            send_sem=column_send_sem,
+            recv_sem=column_sem.at[partner, c],
+            device_id=(d, (partner + nm // 2) % nm),
+            device_id_type=MESH,
+        ).start()
+        return carry
+
+    def send_rows(i, carry):
+        c, part = chunk_at(i)
         for j in range(1, nm):
-            u_copy(near_row, (m + j) % nm).start()
-        here = jnp.logical_and(own_half, k == 0)
-
-        @pl.when(here)
-        def _():
-            pltpu.make_async_copy(
-                u_out.at[m, pl.ds(pl.multiple_of(near_row * rows, rows), rows)],
-                u_in.at[slot],
-                u_recv_sem,
-            ).start()
-
-        @pl.when(jnp.logical_not(here))
-        def _():
-            u_copy(near_row, m).start()
-
-        return carry
-
-    lax.fori_loop(0, per_half // 2, send_u, 0)
+            landed = columns.at[0, 0, part]
+            pltpu.make_async_copy(landed, landed, column_sem.at[(m + j) % nm, c]).wait()
+        for side in range(2):
+            for n in range(chunk_places):
+                near_row = c * chunk_places + (n + d) % chunk_places
+                there = side * per_half + near_row
+                tiles_there = columns.at[side, :, pl.ds(pl.multiple_of(near_row * rows, rows), rows)]
+                place_there = u_in.at[pl.ds(pairs * d, pairs)]
+
+                @pl.when(there == d)
+                def _():
+                    pltpu.make_async_copy(tiles_there, place_there, u_recv_sem).start()
+
+                @pl.when(there != d)
+                def _():
+                    pltpu.make_async_remote_copy(
+                        src_ref=tiles_there,
+                        dst_ref=place_there,
+                        send_sem=u_send_sem,
+                        recv_sem=u_recv_sem,
+                        device_id=(there, m),
+                        device_id_type=MESH,
+                    ).start()
+        return carry
+
+    for k in range(nm):
+        full[:, k * cols : (k + 1) * cols] = slabs[k]
+    pass_on(0, 0)
 
     some_mp = sq_mp.at[pl.ds(0, nm - 1)]
     pltpu.make_async_copy(some_mp, some_mp, sq_recv_sem.at[1]).wait()
@@ -330,10 +380,6 @@
         return carry
 
     lax.fori_loop(1, nd, send_scales, 0)
-    lax.fori_loop(per_half // 2, per_half, send_u, 0)
-
-    for k in range(nm):
-        full[:, k * cols : (k + 1) * cols] = slabs[k]
     loads[2].wait()
 
     def left_gram(n, carry):
@@ -345,6 +391,10 @@
         return carry
 
     lax.fori_loop(0, width // step, left_gram, 0)
+    if chunks > 1:
+        pass_on(1, 0)
+    own_copy.wait()
+    send_rows(0, 0)
     loads[3].wait()
 
     def right_gram(n, carry):
@@ -356,6 +406,14 @@
         return carry
 
     lax.fori_loop(0, width // step, right_gram, 0)
+    if chunks > 1:
+
+        def both(i, carry):
+            pass_on(i + 1, 0)
+            return send_rows(i, carry)
+
+        lax.fori_loop(1, chunks - 1, both, 0)
+        send_rows(chunks - 1, 0)
 
     sent = tiles.at[pl.ds(0, blocks - 1)]
     pltpu.make_async_copy(sent, sent, tile_sem).wait()
@@ -367,14 +425,9 @@
     for j in range(pairs):
         forward(place(j * sigma)).wait_send()
 
-    @pl.when(own_half)
-    def _():
-        pltpu.make_async_copy(sent, sent, u_send_sem).wait()
-
-    @pl.when(jnp.logical_not(own_half))
-    def _():
-        pltpu.make_async_copy(tiles, tiles, u_send_sem).wait()
-
+    sent = tiles.at[pl.ds(0, blocks - pairs)]
+    pltpu.make_async_copy(sent, sent, u_send_sem).wait()
+    pltpu.make_async_copy(u_out, u_out, column_send_sem).wait()
     pltpu.make_async_copy(some, some, sum_recv_sem.at[1]).wait()
     pltpu.make_async_copy(u_in, u_in, u_recv_sem).wait()
 
@@ -437,12 +490,14 @@
             pltpu.VMEM((half, width), F32),
             pltpu.VMEM((half, cols), BF16),
             pltpu.VMEM((nm, half, cols), BF16),
+            pltpu.VMEM((half, cols), BF16),
+            pltpu.VMEM((2, nm // 2, half, cols), BF16),
             pltpu.VMEM((nd, 8, 128), F32),
             pltpu.VMEM((8, 128), F32),
             pltpu.VMEM((nm, 8, 128), F32),
             pltpu.VMEM((8, 128), F32),
             pltpu.VMEM((nm, 8, 128), F32),
-            dma((6,)),
+            dma((7,)),
             dma((nm,)),
             dma,
             dma((nm,)),
@@ -453,6 +508,9 @@
             dma((2,)),
             dma,
             dma,
+            dma((4,)),
+            dma,
+            dma((nm, 4)),
             pltpu.SemaphoreType.REGULAR,
         ],
         compiler_params=pltpu.CompilerParams(

time: 102 us -> 110 us (1.078)
  Pallas kernels: 102 us -> 109 us
    pallas_call x1, Pallas kernels: 99.2 us -> 106 us  [body(): pl.pallas_call(functools.partial(kernel, nd, nm), out_shape=(pltpu.VMEM(l...]
where the time goes in v3:
time: 110 us; the launch traced here: 109 us
  Pallas kernels  109 us (99%)
    pallas_call x1, Pallas kernels, body(): pl.pallas_call(functools.partial(kernel, nd, nm), out_shape=(pltpu.VMEM(l...  106 us
    pallas_call x1, Pallas kernels, body(): pl.pallas_call(finish_kernel, out_shape=(pltpu.HBM(half_shape, F32), pltp...  2.39 us

profile of v3, /device:TPU:1, one launch (start us, length us, event | category | flops | bytes accessed | tf_op | source)
XLA Modules:
  0.0 109.4 jit_solution(7524191369252930695)
XLA Ops:
  0.6 106.3 %step.1 = (f32[1,512,1024]{2,1,0:T(8,128)S(1)}, f32[1,512,1024]{2,1,0:T(8,128)S(1)}, bf16[128,32,128]{2,1,0:T(8,128)(2,1)S(1)}, f32[32,8,128]{2,1,0:T(8,128)S(1)}) custom-call(s32[1,128]{1,0:T(1,128)} %bitcast.1, bf16[128,32,128]{2,1,0:T(8,128)(2,1)} %grads_in.1, f32[1,512,1024]{2,1,0:T(8,128)} %left_stat.1, f32[1,512,1024]{2,1,0:T(8,128)} %right_stat.1, ...), custom_call_target="tpu_custom_call" | custom-call | flops 4294967296 | bytes 12582912 | tf_op jit(solution)/shard_map/step/pallas_call | solution.py:472
  107.0 2.4 %finish.1 = (f32[1,512,1024]{2,1,0:T(8,128)}, f32[1,512,1024]{2,1,0:T(8,128)}, bf16[128,32,128]{2,1,0:T(8,128)(2,1)}) custom-call(s32[1,128]{1,0:T(1,128)} %bitcast.2, f32[1,512,1024]{2,1,0:T(8,128)S(1)} %get-tuple-element.7.left, f32[1,512,1024]{2,1,0:T(8,128)S(1)} %get-tuple-element.8.right, bf16[128,32,128]{2,1,0:T(8,128)(2,1)S(1)} %get-tuple-element.9.tiles, ...), custom_call_target="tpu_custom_call" | custom-call | bytes 5242880 | tf_op jit(solution)/shard_map/finish/pallas_call | solution.py:524

commit v4 on v1

--- a/solution.py
+++ b/solution.py
@@ -36,6 +36,7 @@
     new_right,
     u_in,
     scales,
+    order_row,
     order,
     grads,
     tiles,
@@ -43,8 +44,7 @@
     full,
     lroot,
     rroot,
-    acc,
-    last_a,
+    product,
     u_out,
     sq_dp,
     sq_mine,
@@ -55,6 +55,7 @@
     slab_sem,
     tile_sem,
     forward_sem,
+    root_send_sem,
     root_sem,
     sq_send_sem,
     sq_recv_sem,
@@ -82,6 +83,7 @@
     first_loads = [
         pltpu.make_async_copy(order_in.at[0], order, load_sem.at[4]),
         pltpu.make_async_copy(grads_in, grads, load_sem.at[5]),
+        pltpu.make_async_copy(order_in, order_row, load_sem.at[6]),
     ]
     for load in first_loads:
         load.start()
@@ -107,14 +109,13 @@
     for k in range(1, nm):
         pl.semaphore_signal(ready_sem, inc=1, device_id=(d, (m + k) % nm), device_id_type=MESH)
 
-    part_rows = half // 4
-
-    def root_copy(n):
+    def root_copy(i):
+        part = pl.ds(i * cols, cols)
         return pltpu.make_async_remote_copy(
-            src_ref=right_root.at[0, pl.ds(n * part_rows, part_rows)],
-            dst_ref=rroot.at[pl.ds(pl.multiple_of(h * half + n * part_rows, part_rows), part_rows)],
-            send_sem=root_sem.at[0],
-            recv_sem=root_sem.at[1],
+            src_ref=right_root.at[0, :, part],
+            dst_ref=rroot.at[my_rows, part],
+            send_sem=root_send_sem,
+            recv_sem=root_sem,
             device_id=(d, partner),
             device_id_type=MESH,
         )
@@ -143,7 +144,7 @@
             total = total + fold(tile)
         return total
 
-    for load in first_loads:
+    for load in first_loads[:2]:
         load.wait()
     pl.semaphore_wait(ready_sem, nm - 1)
     total = arrange(d, jnp.zeros((8, 128), F32))
@@ -162,10 +163,11 @@
             tile_copy(there, target).start()
         return total
 
-    sq_dp[d] = lax.fori_loop(1, nd, send_tiles, total)
-
-    for n in range(1, 4):
-        root_copy(n).start()
+    for i in range(pairs):
+        if i > 0:
+            root_copy(i).start()
+        total = lax.fori_loop(max(1, i * nd // pairs), (i + 1) * nd // pairs, send_tiles, total)
+    sq_dp[d] = total
 
     def send_sq(k, carry):
         pltpu.make_async_remote_copy(
@@ -210,52 +212,95 @@
         k = place(j * sigma)
         wait_slab(k)
         forward(k).start()
+        root_copy(pairs + j).start()
 
     loads[0].wait()
-    loads[1].wait()
-    pltpu.make_async_copy(lroot, lroot, root_sem.at[1]).wait()
-    acc[...] = jnp.zeros_like(acc)
     g_sq[...] = jnp.zeros_like(g_sq)
 
     def through_left(k):
         slab = slabs[k]
+        a = jnp.dot(lroot[...], slab, preferred_element_type=F32).astype(BF16)
+        product[:, pl.ds(pl.multiple_of(k * cols, cols), cols)] = a
         g_sq[...] += fold(slab)
-        return jnp.dot(lroot[...], slab, preferred_element_type=F32).astype(BF16)
-
-    def right_rows(k):
-        return pl.ds(pl.multiple_of(k * cols, cols), cols)
-
-    def use_slab(k):
-        a = through_left(k)
-        acc[...] += jnp.dot(a, rroot[right_rows(k)], preferred_element_type=F32)
 
     def near(j, carry):
-        use_slab(place(j * sigma))
+        through_left(place(j * sigma))
         return carry
 
     def far(j, carry):
         k = place(-(j + 1) * sigma)
         wait_slab(k)
-        use_slab(k)
+        through_left(k)
         return carry
 
     lax.fori_loop(0, pairs, near, 0)
     lax.fori_loop(0, pairs - 1, far, 0)
     last = place(-pairs * sigma)
     wait_slab(last)
-    last_a[...] = through_left(last)
+    through_left(last)
+    loads[1].wait()
+    pltpu.make_async_copy(lroot, lroot, root_sem).wait()
+
+    slot = pairs * d + pair
+    own_half = d // per_half == h
+
     step = 2 * cols
 
-    def finish(n, total):
-        part = pl.ds(pl.multiple_of(n * step, step), step)
-        u = acc[:, part] + jnp.dot(
-            last_a[...], rroot[right_rows(last), part], preferred_element_type=F32
-        )
+    def chunk(i):
+        n = (pair + (2, 1, 3, 0)[i]) % pairs
+        return n, pl.ds(pl.multiple_of(n * step, step), step)
+
+    def work_out(i):
+        n, part = chunk(i)
+        u = jnp.dot(product[...], rroot[:, part], preferred_element_type=F32)
         u_out[2 * n] = u[:, :cols].astype(BF16)
         u_out[2 * n + 1] = u[:, cols:].astype(BF16)
-        return total + fold(u[:, :cols]) + fold(u[:, cols:])
-
-    u_sq = lax.fori_loop(0, pairs, finish, jnp.zeros((8, 128), F32))
+        return fold(u[:, :cols]) + fold(u[:, cols:])
+
+    def u_copy(near_row, target):
+        return pltpu.make_async_remote_copy(
+            src_ref=u_out.at[target, pl.ds(pl.multiple_of(near_row * rows, rows), rows)],
+            dst_ref=u_in.at[slot],
+            send_sem=u_send_sem,
+            recv_sem=u_recv_sem,
+            device_id=(h * per_half + near_row, target),
+            device_id_type=MESH,
+        )
+
+    def send_far(i):
+        n, _ = chunk(i)
+
+        def send(k, carry):
+            near_row = (d + k) % per_half
+            for side in range(2):
+                u_copy(near_row, 2 * n + side).start()
+            return carry
+
+        lax.fori_loop(0, per_half, send, 0)
+
+    def send_near(k, carry):
+        near_row = (d + k) % per_half
+        u_copy(near_row, partner).start()
+        here = jnp.logical_and(own_half, k == 0)
+
+        @pl.when(here)
+        def _():
+            pltpu.make_async_copy(
+                u_out.at[m, pl.ds(pl.multiple_of(near_row * rows, rows), rows)],
+                u_in.at[slot],
+                u_recv_sem,
+            ).start()
+
+        @pl.when(jnp.logical_not(here))
+        def _():
+            u_copy(near_row, m).start()
+
+        return carry
+
+    u_sq = work_out(0)
+    send_far(0)
+    for i in range(1, pairs):
+        u_sq = u_sq + work_out(i)
 
     row = lax.broadcasted_iota(jnp.int32, (8, 128), 0)
     sums[m] = jnp.where(row < 4, everything(u_sq), everything(g_sq[...]))
@@ -268,42 +313,8 @@
             device_id=(d, (m + k) % nm),
             device_id_type=MESH,
         ).start()
-
-    slot = pairs * d + pair
-
-    def u_copy(near_row, target):
-        return pltpu.make_async_remote_copy(
-            src_ref=u_out.at[target, pl.ds(pl.multiple_of(near_row * rows, rows), rows)],
-            dst_ref=u_in.at[slot],
-            send_sem=u_send_sem,
-            recv_sem=u_recv_sem,
-            device_id=(h * per_half + near_row, target),
-            device_id_type=MESH,
-        )
-
-    own_half = d // per_half == h
-
-    def send_u(k, carry):
-        near_row = (d + k) % per_half
-        for j in range(1, nm):
-            u_copy(near_row, (m + j) % nm).start()
-        here = jnp.logical_and(own_half, k == 0)
-
-        @pl.when(here)
-        def _():
-            pltpu.make_async_copy(
-                u_out.at[m, pl.ds(pl.multiple_of(near_row * rows, rows), rows)],
-                u_in.at[slot],
-                u_recv_sem,
-            ).start()
-
-        @pl.when(jnp.logical_not(here))
-        def _():
-            u_copy(near_row, m).start()
-
-        return carry
-
-    lax.fori_loop(0, per_half // 2, send_u, 0)
+    for i in range(1, pairs - 1):
+        send_far(i)
 
     some_mp = sq_mp.at[pl.ds(0, nm - 1)]
     pltpu.make_async_copy(some_mp, some_mp, sq_recv_sem.at[1]).wait()
@@ -330,7 +341,7 @@
         return carry
 
     lax.fori_loop(1, nd, send_scales, 0)
-    lax.fori_loop(per_half // 2, per_half, send_u, 0)
+    lax.fori_loop(0, per_half, send_near, 0)
 
     for k in range(nm):
         full[:, k * cols : (k + 1) * cols] = slabs[k]
@@ -357,9 +368,10 @@
 
     lax.fori_loop(0, width // step, right_gram, 0)
 
+    first_loads[2].wait()
     sent = tiles.at[pl.ds(0, blocks - 1)]
     pltpu.make_async_copy(sent, sent, tile_sem).wait()
-    pltpu.make_async_copy(lroot, lroot, root_sem.at[0]).wait()
+    pltpu.make_async_copy(lroot, lroot, root_send_sem).wait()
     pltpu.make_async_copy(some, some, sq_send_sem.at[0]).wait()
     pltpu.make_async_copy(some_mp, some_mp, sq_send_sem.at[1]).wait()
     pltpu.make_async_copy(some_mp, some_mp, sum_send_sem.at[0]).wait()
@@ -379,16 +391,17 @@
     pltpu.make_async_copy(u_in, u_in, u_recv_sem).wait()
 
 
-def finish_kernel(order_in, left, right, tiles, scales, new_left, new_right, update, order, arranged, sem):
-    blocks = tiles.shape[0]
-    pairs = blocks // scales.shape[0]
+def finish_kernel(left, right, tiles, scales, order_in, new_left, new_right, update, order, arranged, sem):
+    places = scales.shape[0]
+    pairs = tiles.shape[0] // places
     order_copy = pltpu.make_async_copy(order_in.at[0], order, sem.at[0])
     order_copy.start()
     stores = [
         pltpu.make_async_copy(left, new_left, sem.at[1]),
         pltpu.make_async_copy(right, new_right, sem.at[2]),
+        pltpu.make_async_copy(arranged, update, sem.at[3]),
     ]
-    for store in stores:
+    for store in stores[:2]:
         store.start()
     order_copy.wait()
 
@@ -398,10 +411,8 @@
             arranged[order[s]] = (tiles[s].astype(F32) * scales[there, p : p + 1]).astype(BF16)
         return carry
 
-    lax.fori_loop(0, scales.shape[0], give, 0, unroll=2)
-    last = pltpu.make_async_copy(arranged, update, sem.at[3])
-    last.start()
-    last.wait()
+    lax.fori_loop(0, places, give, 0, unroll=2)
+    stores[2].start()
     for store in stores:
         store.wait()
 
@@ -423,9 +434,10 @@
             pltpu.VMEM(right_stat.shape, F32),
             pltpu.VMEM(grads.shape, BF16),
             pltpu.VMEM((nd, 8, 128), F32),
+            pltpu.VMEM((1, blocks), jnp.int32),
         ),
         in_specs=[hbm] * 6,
-        out_specs=(vmem, vmem, vmem, vmem),
+        out_specs=(vmem,) * 5,
         scratch_shapes=[
             pltpu.SMEM((blocks,), jnp.int32),
             pltpu.VMEM((blocks, rows, cols), BF16),
@@ -434,19 +446,19 @@
             pltpu.VMEM((width, width), BF16),
             pltpu.VMEM((half, width), BF16),
             pltpu.VMEM((width, width), BF16),
-            pltpu.VMEM((half, width), F32),
-            pltpu.VMEM((half, cols), BF16),
+            pltpu.VMEM((half, width), BF16),
             pltpu.VMEM((nm, half, cols), BF16),
             pltpu.VMEM((nd, 8, 128), F32),
             pltpu.VMEM((8, 128), F32),
             pltpu.VMEM((nm, 8, 128), F32),
             pltpu.VMEM((8, 128), F32),
             pltpu.VMEM((nm, 8, 128), F32),
-            dma((6,)),
+            dma((7,)),
             dma((nm,)),
             dma,
             dma((nm,)),
-            dma((2,)),
+            dma,
+            dma,
             dma((2,)),
             dma((2,)),
             dma((2,)),
@@ -470,7 +482,7 @@
             pltpu.HBM(half_shape, F32),
             pltpu.HBM(grads.shape, BF16),
         ),
-        in_specs=[hbm, vmem, vmem, vmem, vmem],
+        in_specs=[vmem] * 5,
         out_specs=(hbm, hbm, hbm),
         scratch_shapes=[
             pltpu.SMEM((blocks,), jnp.int32),
@@ -480,7 +492,7 @@
         compiler_params=pltpu.CompilerParams(vmem_limit_bytes=8 * 1024 * 1024),
         cost_estimate=pl.CostEstimate(flops=0, bytes_accessed=10 * half * width, transcendentals=0),
         name="finish",
-    )(operands[0], *results)
+    )(*results)
 
 
 def solution(mesh):

time: 102 us -> 102 us (level)
  no operation moved by 1% of the time
where the time goes in v4:
time: 102 us
  Pallas kernels  102 us (100%)
    pallas_call x1, Pallas kernels, body(): pl.pallas_call(functools.partial(kernel, nd, nm), out_shape=(pltpu.VMEM(l...  99.2 us
    pallas_call x1, Pallas kernels, body(): pl.pallas_call(finish_kernel, out_shape=(pltpu.HBM(half_shape, F32), pltp...  2.39 us

profile of v4, /device:TPU:1, one launch (start us, length us, event | category | flops | bytes accessed | tf_op | source)
XLA Modules:
  0.0 102.2 jit_solution(14112889270787998483)
XLA Ops:
  0.6 99.2 %step.1 = (f32[1,512,1024]{2,1,0:T(8,128)S(1)}, f32[1,512,1024]{2,1,0:T(8,128)S(1)}, bf16[128,32,128]{2,1,0:T(8,128)(2,1)S(1)}, f32[32,8,128]{2,1,0:T(8,128)S(1)}, s32[1,128]{1,0:T(1,128)S(1)}) custom-call(s32[1,128]{1,0:T(1,128)} %bitcast.1, bf16[128,32,128]{2,1,0:T(8,128)(2,1)} %grads_in.1, f32[1,512,1024]{2,1,0:T(8,128)} %left_stat.1, ...), custom_call_target="tpu_custom_call" | custom-call | flops 4294967296 | bytes 12582912 | tf_op jit(solution)/shard_map/step/pallas_call | solution.py:430
  99.8 2.4 %finish.1 = (f32[1,512,1024]{2,1,0:T(8,128)}, f32[1,512,1024]{2,1,0:T(8,128)}, bf16[128,32,128]{2,1,0:T(8,128)(2,1)}) custom-call(f32[1,512,1024]{2,1,0:T(8,128)S(1)} %get-tuple-element.8.left, f32[1,512,1024]{2,1,0:T(8,128)S(1)} %get-tuple-element.9.right, bf16[128,32,128]{2,1,0:T(8,128)(2,1)S(1)} %get-tuple-element.10.tiles, ...), custom_call_target="tpu_custom_call" | custom-call | bytes 5242880 | tf_op jit(solution)/shard_map/finish/pallas_call | solution.py:478

commit v5 on v2

--- a/solution.py
+++ b/solution.py
@@ -158,7 +158,7 @@
     ).start()
 
     def send_tiles(k, total):
-        there = (d + k) % nd
+        there = (d + 11 * k) % nd
         total = arrange(there, total)
         for target in targets:
             tile_copy(there, target).start()
@@ -299,7 +299,7 @@
     own_half = d // per_half == h
 
     def send_u(k, carry):
-        near_row = (d + k) % per_half
+        near_row = (d + 7 * k) % per_half
         for j in range(1, nm):
             if j != nm // 2:
                 u_copy(near_row, (m + j) % nm).start()
@@ -323,7 +323,7 @@
     relay_copy.wait_recv()
 
     def pass_on(k, carry):
-        near_row = (d + k) % per_half
+        near_row = (d + 7 * k) % per_half
         pltpu.make_async_remote_copy(
             src_ref=relay.at[pl.ds(pl.multiple_of(near_row * rows, rows), rows)],
             dst_ref=u_in.at[slot],

time: 101 us -> 101 us (level)
  no operation moved by 1% of the time
where the time goes in v5:
time: 101 us; the launch traced here: 100 us
  Pallas kernels  99.8 us (99%)
    pallas_call x1, Pallas kernels, body(): pl.pallas_call(functools.partial(kernel, nd, nm), out_shape=(pltpu.VMEM(l...  97.4 us
    pallas_call x1, Pallas kernels, body(): pl.pallas_call(finish_kernel, out_shape=(pltpu.HBM(half_shape, F32), pltp...  2.39 us

profile of v5, /device:TPU:1, one launch (start us, length us, event | category | flops | bytes accessed | tf_op | source)
XLA Modules:
  0.0 100.5 jit_solution(5652641747257329287)
XLA Ops:
  0.6 97.4 %step.1 = (f32[1,512,1024]{2,1,0:T(8,128)S(1)}, f32[1,512,1024]{2,1,0:T(8,128)S(1)}, bf16[128,32,128]{2,1,0:T(8,128)(2,1)S(1)}, f32[32,8,128]{2,1,0:T(8,128)S(1)}) custom-call(s32[1,128]{1,0:T(1,128)} %bitcast.1, bf16[128,32,128]{2,1,0:T(8,128)(2,1)} %grads_in.1, f32[1,512,1024]{2,1,0:T(8,128)} %left_stat.1, f32[1,512,1024]{2,1,0:T(8,128)} %right_stat.1, ...), custom_call_target="tpu_custom_call" | custom-call | flops 4294967296 | bytes 12582912 | tf_op jit(solution)/shard_map/step/pallas_call | solution.py:451
  98.1 2.4 %finish.1 = (f32[1,512,1024]{2,1,0:T(8,128)}, f32[1,512,1024]{2,1,0:T(8,128)}, bf16[128,32,128]{2,1,0:T(8,128)(2,1)}) custom-call(s32[1,128]{1,0:T(1,128)} %bitcast.2, f32[1,512,1024]{2,1,0:T(8,128)S(1)} %get-tuple-element.7.left, f32[1,512,1024]{2,1,0:T(8,128)S(1)} %get-tuple-element.8.right, bf16[128,32,128]{2,1,0:T(8,128)(2,1)S(1)} %get-tuple-element.9.tiles, ...), custom_call_target="tpu_custom_call" | custom-call | bytes 5242880 | tf_op jit(solution)/shard_map/finish/pallas_call | solution.py:500

commit v6 on v5

--- a/solution.py
+++ b/solution.py
@@ -127,12 +127,17 @@
 
     targets = [place(3 * sigma), place(-2 * sigma), place(sigma), m]
 
+    groups = min(4, nd)
+    group_places = nd // groups
+    group_rows = width // groups
+    group = d // group_places
+
     def tile_copy(there, target):
         return pltpu.make_async_remote_copy(
             src_ref=tiles.at[pairs * there + target // 2],
             dst_ref=slabs.at[m, pl.ds(pl.multiple_of(d * rows, rows), rows)],
             send_sem=tile_sem,
-            recv_sem=slab_sem.at[m],
+            recv_sem=slab_sem.at[m, group],
             device_id=(there, target),
             device_id_type=MESH,
         )
@@ -154,11 +159,12 @@
     pltpu.make_async_copy(
         tiles.at[pairs * d + pair],
         slabs.at[m, pl.ds(pl.multiple_of(d * rows, rows), rows)],
-        slab_sem.at[m],
+        slab_sem.at[m, group],
     ).start()
 
     def send_tiles(k, total):
-        there = (d + 11 * k) % nd
+        there_group = (group - k // group_places + groups) % groups
+        there = there_group * group_places + (d + 3 * k) % group_places
         total = arrange(there, total)
         for target in targets:
             tile_copy(there, target).start()
@@ -195,23 +201,32 @@
             device_id_type=MESH,
         ).start()
 
+    def part_of(k, g):
+        return slabs.at[k, pl.ds(pl.multiple_of(g * group_rows, group_rows), group_rows)]
+
+    def wait_part(k, g):
+        pltpu.make_async_copy(part_of(k, g), part_of(k, g), slab_sem.at[k, g]).wait()
+
     def wait_slab(k):
-        pltpu.make_async_copy(slabs.at[k], slabs.at[k], slab_sem.at[k]).wait()
-
-    def forward(k):
-        return pltpu.make_async_remote_copy(
-            src_ref=slabs.at[k],
-            dst_ref=slabs.at[k],
-            send_sem=forward_sem.at[k],
-            recv_sem=slab_sem.at[k],
-            device_id=(d, partner),
-            device_id_type=MESH,
-        )
-
-    for j in range(pairs):
-        k = place(j * sigma)
-        wait_slab(k)
-        forward(k).start()
+        for g in range(groups):
+            wait_part(k, g)
+
+    def forward(c, carry):
+        g = (group + c) % groups
+        for j in range(pairs):
+            k = place(j * sigma)
+            wait_part(k, g)
+            pltpu.make_async_remote_copy(
+                src_ref=part_of(k, g),
+                dst_ref=part_of(k, g),
+                send_sem=forward_sem,
+                recv_sem=slab_sem.at[k, g],
+                device_id=(d, partner),
+                device_id_type=MESH,
+            ).start()
+        return carry
+
+    lax.fori_loop(0, groups, forward, 0)
 
     loads[0].wait()
     loads[1].wait()
@@ -259,6 +274,18 @@
         u_out[2 * n] = u[:, :cols].astype(BF16)
         u_out[2 * n + 1] = u[:, cols:].astype(BF16)
         return total + fold(u[:, :cols]) + fold(u[:, cols:])
+
+    slot = pairs * d + pair
+
+    def u_copy(near_row, target):
+        return pltpu.make_async_remote_copy(
+            src_ref=u_out.at[target, pl.ds(pl.multiple_of(near_row * rows, rows), rows)],
+            dst_ref=u_in.at[slot],
+            send_sem=u_send_sem,
+            recv_sem=u_recv_sem,
+            device_id=(h * per_half + near_row, target),
+            device_id_type=MESH,
+        )
 
     u_sq = finish(0, jnp.zeros((8, 128), F32))
     relay_copy = pltpu.make_async_remote_copy(
@@ -270,6 +297,13 @@
         device_id_type=MESH,
     )
     relay_copy.start()
+    beside = place(3 * sigma)
+
+    def send_beside(k, carry):
+        u_copy((d + 7 * k) % per_half, beside).start()
+        return carry
+
+    lax.fori_loop(0, per_half, send_beside, 0)
     u_sq = lax.fori_loop(1, pairs, finish, u_sq)
 
     row = lax.broadcasted_iota(jnp.int32, (8, 128), 0)
@@ -284,25 +318,12 @@
             device_id_type=MESH,
         ).start()
 
-    slot = pairs * d + pair
-
-    def u_copy(near_row, target):
-        return pltpu.make_async_remote_copy(
-            src_ref=u_out.at[target, pl.ds(pl.multiple_of(near_row * rows, rows), rows)],
-            dst_ref=u_in.at[slot],
-            send_sem=u_send_sem,
-            recv_sem=u_recv_sem,
-            device_id=(h * per_half + near_row, target),
-            device_id_type=MESH,
-        )
-
     own_half = d // per_half == h
 
     def send_u(k, carry):
         near_row = (d + 7 * k) % per_half
-        for j in range(1, nm):
-            if j != nm // 2:
-                u_copy(near_row, (m + j) % nm).start()
+        for j in (-3, 2, -2, 1, -1):
+            u_copy(near_row, place(j * sigma)).start()
         here = jnp.logical_and(own_half, k == 0)
 
         @pl.when(here)
@@ -396,8 +417,7 @@
     pltpu.make_async_copy(some_mp, some_mp, sum_send_sem.at[0]).wait()
     pltpu.make_async_copy(some, some, sum_send_sem.at[1]).wait()
     relay_copy.wait_send()
-    for j in range(pairs):
-        forward(place(j * sigma)).wait_send()
+    pltpu.make_async_copy(lroot, lroot, forward_sem).wait()
 
     @pl.when(own_half)
     def _():
@@ -476,9 +496,9 @@
             pltpu.VMEM((8, 128), F32),
             pltpu.VMEM((nm, 8, 128), F32),
             dma((6,)),
-            dma((nm,)),
+            dma((nm, 4)),
             dma,
-            dma((nm,)),
+            dma,
             dma((2,)),
             dma((2,)),
             dma((2,)),

time: 101 us -> 101 us (level)
  no operation moved by 1% of the time
where the time goes in v6:
time: 101 us
  Pallas kernels  100 us (99%)
    pallas_call x1, Pallas kernels, body(): pl.pallas_call(functools.partial(kernel, nd, nm), out_shape=(pltpu.VMEM(l...  97.6 us
    pallas_call x1, Pallas kernels, body(): pl.pallas_call(finish_kernel, out_shape=(pltpu.HBM(half_shape, F32), pltp...  2.39 us

profile of v6, /device:TPU:1, one launch (start us, length us, event | category | flops | bytes accessed | tf_op | source)
XLA Modules:
  0.0 100.7 jit_solution(8603590518786277343)
XLA Ops:
  0.6 97.6 %step.1 = (f32[1,512,1024]{2,1,0:T(8,128)S(1)}, f32[1,512,1024]{2,1,0:T(8,128)S(1)}, bf16[128,32,128]{2,1,0:T(8,128)(2,1)S(1)}, f32[32,8,128]{2,1,0:T(8,128)S(1)}) custom-call(s32[1,128]{1,0:T(1,128)} %bitcast.1, bf16[128,32,128]{2,1,0:T(8,128)(2,1)} %grads_in.1, f32[1,512,1024]{2,1,0:T(8,128)} %left_stat.1, f32[1,512,1024]{2,1,0:T(8,128)} %right_stat.1, ...), custom_call_target="tpu_custom_call" | custom-call | flops 4294967296 | bytes 12582912 | tf_op jit(solution)/shard_map/step/pallas_call | solution.py:471
  98.3 2.4 %finish.1 = (f32[1,512,1024]{2,1,0:T(8,128)}, f32[1,512,1024]{2,1,0:T(8,128)}, bf16[128,32,128]{2,1,0:T(8,128)(2,1)}) custom-call(s32[1,128]{1,0:T(1,128)} %bitcast.2, f32[1,512,1024]{2,1,0:T(8,128)S(1)} %get-tuple-element.7.left, f32[1,512,1024]{2,1,0:T(8,128)S(1)} %get-tuple-element.8.right, bf16[128,32,128]{2,1,0:T(8,128)(2,1)S(1)} %get-tuple-element.9.tiles, ...), custom_call_target="tpu_custom_call" | custom-call | bytes 5242880 | tf_op jit(solution)/shard_map/finish/pallas_call | solution.py:520

commit v7 on v6

--- a/solution.py
+++ b/solution.py
@@ -36,7 +36,9 @@
     new_right,
     u_in,
     scales,
+    inverse,
     order,
+    order_row,
     grads,
     tiles,
     slabs,
@@ -84,6 +86,7 @@
     first_loads = [
         pltpu.make_async_copy(order_in.at[0], order, load_sem.at[4]),
         pltpu.make_async_copy(grads_in, grads, load_sem.at[5]),
+        pltpu.make_async_copy(order_in, order_row, load_sem.at[6]),
     ]
     for load in first_loads:
         load.start()
@@ -228,6 +231,11 @@
 
     lax.fori_loop(0, groups, forward, 0)
 
+    spread = jnp.transpose(jnp.broadcast_to(order_row[...], (blocks, blocks)))
+    slot_of = lax.broadcasted_iota(jnp.int32, (blocks, blocks), 0)
+    block_of = lax.broadcasted_iota(jnp.int32, (blocks, blocks), 1)
+    inverse[...] = jnp.max(jnp.where(spread == block_of, slot_of, 0), axis=0, keepdims=True)
+
     loads[0].wait()
     loads[1].wait()
     pltpu.make_async_copy(lroot, lroot, root_sem.at[1]).wait()
@@ -431,29 +439,41 @@
     pltpu.make_async_copy(u_in, u_in, u_recv_sem).wait()
 
 
-def finish_kernel(order_in, left, right, tiles, scales, new_left, new_right, update, order, arranged, sem):
+def finish_kernel(
+    left, right, tiles, scales, inverse_in, new_left, new_right, update, inverse, scaled, arranged, sem
+):
+    places = scales.shape[0]
     blocks = tiles.shape[0]
-    pairs = blocks // scales.shape[0]
-    order_copy = pltpu.make_async_copy(order_in.at[0], order, sem.at[0])
-    order_copy.start()
+    pairs = blocks // places
+    inverse_copy = pltpu.make_async_copy(inverse_in.at[0], inverse, sem.at[0])
+    inverse_copy.start()
     stores = [
         pltpu.make_async_copy(left, new_left, sem.at[1]),
         pltpu.make_async_copy(right, new_right, sem.at[2]),
     ]
     for store in stores:
         store.start()
-    order_copy.wait()
-
-    def give(there, carry):
+
+    def scale(there, carry):
         for p in range(pairs):
             s = pairs * there + p
-            arranged[order[s]] = (tiles[s].astype(F32) * scales[there, p : p + 1]).astype(BF16)
-        return carry
-
-    lax.fori_loop(0, scales.shape[0], give, 0, unroll=2)
-    last = pltpu.make_async_copy(arranged, update, sem.at[3])
-    last.start()
-    last.wait()
+            scaled[s] = (tiles[s].astype(F32) * scales[there, p : p + 1]).astype(BF16)
+        return carry
+
+    lax.fori_loop(0, places, scale, 0, unroll=2)
+    inverse_copy.wait()
+
+    def give(b, carry):
+        arranged[b] = scaled[inverse[b]]
+        return carry
+
+    parts = 4
+    size = blocks // parts
+    for n in range(parts):
+        lax.fori_loop(n * size, (n + 1) * size, give, 0, unroll=min(8, size))
+        part = pl.ds(n * size, size)
+        stores.append(pltpu.make_async_copy(arranged.at[part], update.at[part], sem.at[3 + n]))
+        stores[-1].start()
     for store in stores:
         store.wait()
 
@@ -475,11 +495,13 @@
             pltpu.VMEM(right_stat.shape, F32),
             pltpu.VMEM(grads.shape, BF16),
             pltpu.VMEM((nd, 8, 128), F32),
+            pltpu.VMEM((1, blocks), jnp.int32),
         ),
         in_specs=[hbm] * 6,
-        out_specs=(vmem, vmem, vmem, vmem),
+        out_specs=(vmem,) * 5,
         scratch_shapes=[
             pltpu.SMEM((blocks,), jnp.int32),
+            pltpu.VMEM((1, blocks), jnp.int32),
             pltpu.VMEM((blocks, rows, cols), BF16),
             pltpu.VMEM((blocks, rows, cols), BF16),
             pltpu.VMEM((nm, width, cols), BF16),
@@ -495,7 +517,7 @@
             pltpu.VMEM((nm, 8, 128), F32),
             pltpu.VMEM((8, 128), F32),
             pltpu.VMEM((nm, 8, 128), F32),
-            dma((6,)),
+            dma((7,)),
             dma((nm, 4)),
             dma,
             dma,
@@ -524,17 +546,18 @@
             pltpu.HBM(half_shape, F32),
             pltpu.HBM(grads.shape, BF16),
         ),
-        in_specs=[hbm, vmem, vmem, vmem, vmem],
+        in_specs=[vmem] * 5,
         out_specs=(hbm, hbm, hbm),
         scratch_shapes=[
             pltpu.SMEM((blocks,), jnp.int32),
             pltpu.VMEM(grads.shape, BF16),
-            dma((4,)),
+            pltpu.VMEM(grads.shape, BF16),
+            dma((7,)),
         ],
         compiler_params=pltpu.CompilerParams(vmem_limit_bytes=8 * 1024 * 1024),
         cost_estimate=pl.CostEstimate(flops=0, bytes_accessed=10 * half * width, transcendentals=0),
         name="finish",
-    )(operands[0], *results)
+    )(*results)
 
 
 def solution(mesh):

time: 101 us -> 101 us (level)
  no operation moved by 1% of the time
where the time goes in v7:
time: 101 us
  Pallas kernels  100 us (99%)
    pallas_call x1, Pallas kernels, body(): pl.pallas_call(functools.partial(kernel, nd, nm), out_shape=(pltpu.VMEM(l...  97.6 us
    pallas_call x1, Pallas kernels, body(): pl.pallas_call(finish_kernel, out_shape=(pltpu.HBM(half_shape, F32), pltp...  2.38 us

profile of v7, /device:TPU:1, one launch (start us, length us, event | category | flops | bytes accessed | tf_op | source)
XLA Modules:
  0.0 100.7 jit_solution(9985973423052270072)
XLA Ops:
  0.6 97.6 %step.1 = (f32[1,512,1024]{2,1,0:T(8,128)S(1)}, f32[1,512,1024]{2,1,0:T(8,128)S(1)}, bf16[128,32,128]{2,1,0:T(8,128)(2,1)S(1)}, f32[32,8,128]{2,1,0:T(8,128)S(1)}, s32[1,128]{1,0:T(1,128)S(1)}) custom-call(s32[1,128]{1,0:T(1,128)} %bitcast.1, bf16[128,32,128]{2,1,0:T(8,128)(2,1)} %grads_in.1, f32[1,512,1024]{2,1,0:T(8,128)} %left_stat.1, ...), custom_call_target="tpu_custom_call" | custom-call | flops 4294967296 | bytes 12582912 | tf_op jit(solution)/shard_map/step/pallas_call | solution.py:491
  98.3 2.4 %finish.1 = (f32[1,512,1024]{2,1,0:T(8,128)}, f32[1,512,1024]{2,1,0:T(8,128)}, bf16[128,32,128]{2,1,0:T(8,128)(2,1)}) custom-call(f32[1,512,1024]{2,1,0:T(8,128)S(1)} %get-tuple-element.8.left, f32[1,512,1024]{2,1,0:T(8,128)S(1)} %get-tuple-element.9.right, bf16[128,32,128]{2,1,0:T(8,128)(2,1)S(1)} %get-tuple-element.10.tiles, ...), custom_call_target="tpu_custom_call" | custom-call | bytes 5242880 | tf_op jit(solution)/shard_map/finish/pallas_call | solution.py:542

commit v8 on v7

--- a/solution.py
+++ b/solution.py
@@ -328,10 +328,19 @@
 
     own_half = d // per_half == h
 
+    across = opposite // 2 + 1 - 2 * (opposite // 2 % 2)
+    along = pair + 1 - 2 * (pair % 2)
+
+    def send_across(k, carry):
+        near_row = (d + 7 * k) % per_half
+        for side in range(2):
+            u_copy(near_row, 2 * across + side).start()
+        return carry
+
     def send_u(k, carry):
         near_row = (d + 7 * k) % per_half
-        for j in (-3, 2, -2, 1, -1):
-            u_copy(near_row, place(j * sigma)).start()
+        for target in (2 * along, 2 * along + 1, partner):
+            u_copy(near_row, target).start()
         here = jnp.logical_and(own_half, k == 0)
 
         @pl.when(here)
@@ -348,7 +357,7 @@
 
         return carry
 
-    lax.fori_loop(0, per_half // 2, send_u, 0)
+    lax.fori_loop(0, per_half, send_across, 0)
     relay_copy.wait_recv()
 
     def pass_on(k, carry):
@@ -390,7 +399,7 @@
         return carry
 
     lax.fori_loop(1, nd, send_scales, 0)
-    lax.fori_loop(per_half // 2, per_half, send_u, 0)
+    lax.fori_loop(0, per_half, send_u, 0)
 
     for k in range(nm):
         full[:, k * cols : (k + 1) * cols] = slabs[k]
@@ -447,10 +456,13 @@
     pairs = blocks // places
     inverse_copy = pltpu.make_async_copy(inverse_in.at[0], inverse, sem.at[0])
     inverse_copy.start()
-    stores = [
-        pltpu.make_async_copy(left, new_left, sem.at[1]),
-        pltpu.make_async_copy(right, new_right, sem.at[2]),
-    ]
+    parts = 4
+    some = left.shape[1] // parts
+    stores = []
+    for n in range(parts):
+        part = pl.ds(n * some, some)
+        stores.append(pltpu.make_async_copy(left.at[:, part], new_left.at[:, part], sem.at[1 + n]))
+        stores.append(pltpu.make_async_copy(right.at[:, part], new_right.at[:, part], sem.at[1 + parts + n]))
     for store in stores:
         store.start()
 
@@ -467,12 +479,11 @@
         arranged[b] = scaled[inverse[b]]
         return carry
 
-    parts = 4
     size = blocks // parts
     for n in range(parts):
         lax.fori_loop(n * size, (n + 1) * size, give, 0, unroll=min(8, size))
         part = pl.ds(n * size, size)
-        stores.append(pltpu.make_async_copy(arranged.at[part], update.at[part], sem.at[3 + n]))
+        stores.append(pltpu.make_async_copy(arranged.at[part], update.at[part], sem.at[1 + 2 * parts + n]))
         stores[-1].start()
     for store in stores:
         store.wait()
@@ -552,7 +563,7 @@
             pltpu.SMEM((blocks,), jnp.int32),
             pltpu.VMEM(grads.shape, BF16),
             pltpu.VMEM(grads.shape, BF16),
-            dma((7,)),
+            dma((13,)),
         ],
         compiler_params=pltpu.CompilerParams(vmem_limit_bytes=8 * 1024 * 1024),
         cost_estimate=pl.CostEstimate(flops=0, bytes_accessed=10 * half * width, transcendentals=0),

time: 101 us -> 103 us (1.020)
  the two profiles are of different devices: /device:TPU:1 before, /device:TPU:14 now
where the time goes in v8:
time: 103 us
  Pallas kernels  103 us (100%)
    pallas_call x1, Pallas kernels, body(): pl.pallas_call(functools.partial(kernel, nd, nm), out_shape=(pltpu.VMEM(l...  100 us
    pallas_call x1, Pallas kernels, body(): pl.pallas_call(finish_kernel, out_shape=(pltpu.HBM(half_shape, F32), pltp...  2.43 us

profile of v8, /device:TPU:14, one launch (start us, length us, event | category | flops | bytes accessed | tf_op | source)
XLA Modules:
  0.0 103.3 jit_solution(11363226371087519145)
XLA Ops:
  0.6 100.2 %step.1 = (f32[1,512,1024]{2,1,0:T(8,128)S(1)}, f32[1,512,1024]{2,1,0:T(8,128)S(1)}, bf16[128,32,128]{2,1,0:T(8,128)(2,1)S(1)}, f32[32,8,128]{2,1,0:T(8,128)S(1)}, s32[1,128]{1,0:T(1,128)S(1)}) custom-call(s32[1,128]{1,0:T(1,128)} %bitcast.1, bf16[128,32,128]{2,1,0:T(8,128)(2,1)} %grads_in.1, f32[1,512,1024]{2,1,0:T(8,128)} %left_stat.1, ...), custom_call_target="tpu_custom_call" | custom-call | flops 4294967296 | bytes 12582912 | tf_op jit(solution)/shard_map/step/pallas_call | solution.py:502
  100.8 2.4 %finish.1 = (f32[1,512,1024]{2,1,0:T(8,128)}, f32[1,512,1024]{2,1,0:T(8,128)}, bf16[128,32,128]{2,1,0:T(8,128)(2,1)}) custom-call(f32[1,512,1024]{2,1,0:T(8,128)S(1)} %get-tuple-element.8.left, f32[1,512,1024]{2,1,0:T(8,128)S(1)} %get-tuple-element.9.right, bf16[128,32,128]{2,1,0:T(8,128)(2,1)S(1)} %get-tuple-element.10.tiles, ...), custom_call_target="tpu_custom_call" | custom-call | bytes 5242880 | tf_op jit(solution)/shard_map/finish/pallas_call | solution.py:553

commit v9 on v7

--- a/solution.py
+++ b/solution.py
@@ -305,13 +305,6 @@
         device_id_type=MESH,
     )
     relay_copy.start()
-    beside = place(3 * sigma)
-
-    def send_beside(k, carry):
-        u_copy((d + 7 * k) % per_half, beside).start()
-        return carry
-
-    lax.fori_loop(0, per_half, send_beside, 0)
     u_sq = lax.fori_loop(1, pairs, finish, u_sq)
 
     row = lax.broadcasted_iota(jnp.int32, (8, 128), 0)
@@ -330,8 +323,8 @@
 
     def send_u(k, carry):
         near_row = (d + 7 * k) % per_half
-        for j in (-3, 2, -2, 1, -1):
-            u_copy(near_row, place(j * sigma)).start()
+        for i, j in enumerate((3, -3, 2, -2, 1, -1)):
+            u_copy((near_row + 5 * i + 3) % per_half, place(j * sigma)).start()
         here = jnp.logical_and(own_half, k == 0)
 
         @pl.when(here)
@@ -352,7 +345,7 @@
     relay_copy.wait_recv()
 
     def pass_on(k, carry):
-        near_row = (d + 7 * k) % per_half
+        near_row = (d + 7 * k + 1) % per_half
         pltpu.make_async_remote_copy(
             src_ref=relay.at[pl.ds(pl.multiple_of(near_row * rows, rows), rows)],
             dst_ref=u_in.at[slot],
@@ -363,7 +356,6 @@
         ).start()
         return carry
 
-    lax.fori_loop(0, per_half, pass_on, 0)
 
     some_mp = sq_mp.at[pl.ds(0, nm - 1)]
     pltpu.make_async_copy(some_mp, some_mp, sq_recv_sem.at[1]).wait()
@@ -390,7 +382,17 @@
         return carry
 
     lax.fori_loop(1, nd, send_scales, 0)
-    lax.fori_loop(per_half // 2, per_half, send_u, 0)
+
+    def send_both(k, carry):
+        pass_on(2 * k - per_half, 0)
+        send_u(k, carry)
+        return pass_on(2 * k - per_half + 1, carry)
+
+    if per_half % 2:
+        pass_on(0, 0)
+        lax.fori_loop(0, per_half, send_u, 0)
+    else:
+        lax.fori_loop(per_half // 2, per_half, send_both, 0)
 
     for k in range(nm):
         full[:, k * cols : (k + 1) * cols] = slabs[k]

time: 101 us -> 102 us (level)
    pallas_call x1, Pallas kernels: 97.6 us -> 98.7 us  [body(): pl.pallas_call(functools.partial(kernel, nd, nm), out_shape=(pltpu.VMEM(l...]
where the time goes in v9:
time: 102 us
  Pallas kernels  101 us (99%)
    pallas_call x1, Pallas kernels, body(): pl.pallas_call(functools.partial(kernel, nd, nm), out_shape=(pltpu.VMEM(l...  98.7 us
    pallas_call x1, Pallas kernels, body(): pl.pallas_call(finish_kernel, out_shape=(pltpu.HBM(half_shape, F32), pltp...  2.38 us

profile of v9, /device:TPU:1, one launch (start us, length us, event | category | flops | bytes accessed | tf_op | source)
XLA Modules:
  0.0 101.7 jit_solution(11720028151932446724)
XLA Ops:
  0.6 98.7 %step.1 = (f32[1,512,1024]{2,1,0:T(8,128)S(1)}, f32[1,512,1024]{2,1,0:T(8,128)S(1)}, bf16[128,32,128]{2,1,0:T(8,128)(2,1)S(1)}, f32[32,8,128]{2,1,0:T(8,128)S(1)}, s32[1,128]{1,0:T(1,128)S(1)}) custom-call(s32[1,128]{1,0:T(1,128)} %bitcast.1, bf16[128,32,128]{2,1,0:T(8,128)(2,1)} %grads_in.1, f32[1,512,1024]{2,1,0:T(8,128)} %left_stat.1, ...), custom_call_target="tpu_custom_call" | custom-call | flops 4294967296 | bytes 12582912 | tf_op jit(solution)/shard_map/step/pallas_call | solution.py:493
  99.3 2.4 %finish.1 = (f32[1,512,1024]{2,1,0:T(8,128)}, f32[1,512,1024]{2,1,0:T(8,128)}, bf16[128,32,128]{2,1,0:T(8,128)(2,1)}) custom-call(f32[1,512,1024]{2,1,0:T(8,128)S(1)} %get-tuple-element.8.left, f32[1,512,1024]{2,1,0:T(8,128)S(1)} %get-tuple-element.9.right, bf16[128,32,128]{2,1,0:T(8,128)(2,1)S(1)} %get-tuple-element.10.tiles, ...), custom_call_target="tpu_custom_call" | custom-call | bytes 5242880 | tf_op jit(solution)/shard_map/finish/pallas_call | solution.py:544

commit v10 on v7

--- a/solution.py
+++ b/solution.py
@@ -348,7 +348,7 @@
 
         return carry
 
-    lax.fori_loop(0, per_half // 2, send_u, 0)
+    lax.fori_loop(0, per_half // 4, send_u, 0)
     relay_copy.wait_recv()
 
     def pass_on(k, carry):
@@ -364,6 +364,7 @@
         return carry
 
     lax.fori_loop(0, per_half, pass_on, 0)
+    lax.fori_loop(per_half // 4, per_half // 2, send_u, 0)
 
     some_mp = sq_mp.at[pl.ds(0, nm - 1)]
     pltpu.make_async_copy(some_mp, some_mp, sq_recv_sem.at[1]).wait()

time: 101 us -> 101 us (level)
  no operation moved by 1% of the time
where the time goes in v10:
time: 101 us
  Pallas kernels  100 us (99%)
    pallas_call x1, Pallas kernels, body(): pl.pallas_call(functools.partial(kernel, nd, nm), out_shape=(pltpu.VMEM(l...  97.6 us
    pallas_call x1, Pallas kernels, body(): pl.pallas_call(finish_kernel, out_shape=(pltpu.HBM(half_shape, F32), pltp...  2.38 us

profile of v10, /device:TPU:1, one launch (start us, length us, event | category | flops | bytes accessed | tf_op | source)
XLA Modules:
  0.0 100.7 jit_solution(11831653327605170518)
XLA Ops:
  0.6 97.6 %step.1 = (f32[1,512,1024]{2,1,0:T(8,128)S(1)}, f32[1,512,1024]{2,1,0:T(8,128)S(1)}, bf16[128,32,128]{2,1,0:T(8,128)(2,1)S(1)}, f32[32,8,128]{2,1,0:T(8,128)S(1)}, s32[1,128]{1,0:T(1,128)S(1)}) custom-call(s32[1,128]{1,0:T(1,128)} %bitcast.1, bf16[128,32,128]{2,1,0:T(8,128)(2,1)} %grads_in.1, f32[1,512,1024]{2,1,0:T(8,128)} %left_stat.1, ...), custom_call_target="tpu_custom_call" | custom-call | flops 4294967296 | bytes 12582912 | tf_op jit(solution)/shard_map/step/pallas_call | solution.py:492
  98.3 2.4 %finish.1 = (f32[1,512,1024]{2,1,0:T(8,128)}, f32[1,512,1024]{2,1,0:T(8,128)}, bf16[128,32,128]{2,1,0:T(8,128)(2,1)}) custom-call(f32[1,512,1024]{2,1,0:T(8,128)S(1)} %get-tuple-element.8.left, f32[1,512,1024]{2,1,0:T(8,128)S(1)} %get-tuple-element.9.right, bf16[128,32,128]{2,1,0:T(8,128)(2,1)S(1)} %get-tuple-element.10.tiles, ...), custom_call_target="tpu_custom_call" | custom-call | bytes 5242880 | tf_op jit(solution)/shard_map/finish/pallas_call | solution.py:543
